TPU v7x, 256 devices: a whole 4x4x8 slice. The times are simulated.
256 devices in a mesh: pos: 32 (over z_lo, x, core), chan: 8 (over z_hi, y).
Axes of the slice: x: 4, y: 4, z: 8 (z_hi: 2, z_lo: 4; z = z_hi * 4 + z_lo), core: 2. Of those that a mesh axis runs over, the one named last changes fastest.
Arguments:
- prompt_signal: bfloat16 [8192, 8192], P('pos', 'chan'), may hold values from -6 to 6
- long_filter: bfloat16 [2, 8192, 8192], P(None, 'pos', 'chan'), may hold values from -1 to 1, as said below
- sample_tokens: int32 [1024, 4], P('pos'), may hold values from 0 to 255
- token_features: bfloat16 [256, 3, 8192], P(None, None, 'chan'), may hold values from -6 to 6
- out_weight: bfloat16 [8192, 4096], P('chan'), may hold values from -0.0625 to 0.0625
Outputs:
- contributions: bfloat16 [8192, 8192], P('pos', 'chan')
- decoded: bfloat16 [1024, 4, 4096], P('pos', None, 'chan')
Inputs may be any that keep to these rules, and one draw needn't show every extreme that they name: `long_filter`: each entry of the filter lies between the bounds.
All inputs are finite; a program needn't handle non-finite values.
Results may differ from a plain program's by a relative error of at most 0.015.
Values may be sent and summed in bfloat16 or wider, within the bound.
A program may use at most 128 MiB of HBM per device.

v0:
```python
import math

import jax
import jax.numpy as jnp
from jax import lax
from jax.sharding import PartitionSpec as P

precise = lax.Precision.HIGH


def spread(x, axis, root):
    mine = lax.axis_index(axis) == root
    return lax.psum(jnp.where(mine, x, jnp.zeros_like(x)), axis)


def angle_table(first_index, second_index, period):
    product = first_index[:, None] * second_index[None, :] % period
    angles = product.astype(jnp.float32) * (2.0 * math.pi / period)
    return (jnp.cos(angles), -jnp.sin(angles))


def contract(subscripts, matrix, operand):
    return jnp.einsum(
        subscripts, matrix, operand, precision=precise, preferred_element_type=jnp.float32
    )


def split_contract(subscripts, table, operand):
    table_high = table.astype(jnp.bfloat16)
    table_low = (table - table_high.astype(jnp.float32)).astype(jnp.bfloat16)
    high_part = jnp.einsum(subscripts, table_high, operand, preferred_element_type=jnp.float32)
    low_part = jnp.einsum(subscripts, table_low, operand, preferred_element_type=jnp.float32)
    return high_part + low_part


def complex_contract(subscripts, table_re, table_im, value_re, value_im):
    real_part = contract(subscripts, table_re, value_re) - contract(subscripts, table_im, value_im)
    imag_part = contract(subscripts, table_re, value_im) + contract(subscripts, table_im, value_re)
    return (real_part, imag_part)


def per_device(prompt_signal, long_filter, sample_tokens, token_features, out_weight):
    groups = lax.axis_size("pos")
    device_pos = lax.axis_index("pos")
    freqs_outer = 2 * groups
    rows_local = prompt_signal.shape[0]
    channels = prompt_signal.shape[1]
    length = freqs_outer * rows_local
    outer_index = jnp.arange(freqs_outer, dtype=jnp.int32)
    local_index = jnp.arange(rows_local, dtype=jnp.int32)
    cos_outer, sin_outer = angle_table(
        outer_index, jnp.arange(groups, dtype=jnp.int32), freqs_outer
    )
    cos_inner, sin_inner = angle_table(local_index, local_index, rows_local)
    parity = (1 - 2 * (outer_index % 2)).astype(jnp.float32)
    stacked = jnp.concatenate([prompt_signal[None], long_filter], 0)
    block_rows = rows_local // groups
    pieces = lax.all_to_all(stacked[:, None], "pos", split_axis=2, concat_axis=1, tiled=True)
    first_re = split_contract("kp,ipbc->ikbc", cos_outer, pieces)
    first_im = split_contract("kp,ipbc->ikbc", sin_outer, pieces)
    sign_col = parity[:, None, None]
    spec_re = jnp.stack([first_re[0], first_re[1] + sign_col * first_re[2]])
    spec_im = jnp.stack([first_im[0], first_im[1] + sign_col * first_im[2]])
    block_global = device_pos * block_rows + jnp.arange(block_rows, dtype=jnp.int32)
    twid_re, twid_im = angle_table(outer_index, block_global, length)
    twid_re = twid_re[:, :, None]
    twid_im = twid_im[:, :, None]
    turned_re = spec_re * twid_re - spec_im * twid_im
    turned_im = spec_re * twid_im + spec_im * twid_re
    moved = lax.all_to_all(
        jnp.stack([turned_re, turned_im], 1), "pos", split_axis=2, concat_axis=3, tiled=True
    )
    freq_re, freq_im = complex_contract(
        "mb,sjbc->sjmc", cos_inner, sin_inner, moved[:, 0], moved[:, 1]
    )
    prod_re = freq_re[0] * freq_re[1] - freq_im[0] * freq_im[1]
    prod_im = freq_re[0] * freq_im[1] + freq_im[0] * freq_re[1]
    back_re, back_im = complex_contract("mb,jmc->jbc", cos_inner, -sin_inner, prod_re, prod_im)
    owned_freqs = 2 * device_pos + jnp.arange(2, dtype=jnp.int32)
    owned_sign = (1 - 2 * (owned_freqs % 2)).astype(jnp.float32)[:, None, None]
    undo_re, undo_im = angle_table(owned_freqs, local_index, length)
    undo_re = owned_sign * undo_re[:, :, None]
    undo_im = -owned_sign * undo_im[:, :, None]
    final_re = back_re * undo_re - back_im * undo_im
    final_im = back_re * undo_im + back_im * undo_re
    regrouped = lax.all_to_all(
        jnp.stack([final_re, final_im]), "pos", split_axis=2, concat_axis=1, tiled=True
    )
    result = (
        contract("kp,kbc->pbc", cos_outer, regrouped[0])
        + contract("kp,kbc->pbc", sin_outer, regrouped[1])
    ) / length
    returned = lax.all_to_all(
        result.astype(jnp.bfloat16), "pos", split_axis=0, concat_axis=1, tiled=True
    )
    signal_rows = returned.reshape(rows_local, channels)
    samples = sample_tokens.shape[0]
    steps = sample_tokens.shape[1]
    vocab = token_features.shape[0]
    onehot = (
        sample_tokens.reshape(-1)[:, None] == jnp.arange(vocab, dtype=jnp.int32)[None, :]
    ).astype(jnp.bfloat16)
    looked = jnp.dot(
        onehot, token_features.reshape(vocab, 3 * channels), preferred_element_type=jnp.float32
    )
    looked = looked.reshape(samples, steps, 3, channels)
    query = looked[:, :, 0]
    own = looked[:, :, 1] * looked[:, :, 2]
    seeds = spread(jnp.concatenate([signal_rows[:steps], long_filter[0, :steps]], 0), "pos", 0)
    seed_rows = seeds[:steps].astype(jnp.float32)
    filt_head = seeds[steps:].astype(jnp.float32)
    columns = []
    for current in range(steps):
        mixed = jnp.broadcast_to(seed_rows[current], own[:, current].shape)
        for earlier in range(current + 1):
            mixed = mixed + filt_head[current - earlier] * own[:, earlier]
        columns.append(mixed)
    mixed_all = jnp.stack(columns, 1)
    gated = (query * mixed_all).astype(jnp.bfloat16)
    terms = jnp.dot(gated.reshape(-1, channels), out_weight, preferred_element_type=jnp.float32)
    terms = terms.reshape(samples, steps, out_weight.shape[1])
    decoded = lax.psum_scatter(terms, "chan", scatter_dimension=2, tiled=True).astype(jnp.bfloat16)
    return (signal_rows, decoded)


def solution(mesh):
    placed = (
        P("pos", "chan"),
        P(None, "pos", "chan"),
        P("pos", None),
        P(None, None, "chan"),
        P("chan", None),
    )
    return jax.shard_map(
        per_device,
        mesh=mesh,
        in_specs=placed,
        out_specs=(P("pos", "chan"), P("pos", None, "chan")),
        check_vma=False,
    )
```

profile of v0, /device:TPU:6, one launch (start us, length us, event | category | flops | bytes accessed | tf_op | source)
XLA Modules:
  0.0 726.0 jit_solution(9673467790690082780)
XLA Ops:
  7.2 0.0 copy-start.2
  7.2 1.9 copy.43
  9.1 0.0 copy-done.2
  9.1 1.1 copy.44
  10.2 3.2 maximum_bitcast_fusion
  13.4 9.3 %all-to-all-start = ((bf16[3,1,256,1024]{3,0,1,2:T(4,128)(2,1)}), bf16[3,1,256,1024]{3,0,1,2:T(4,128)(2,1)S(1)}, u32[]{:S(2)}, u32[]{:S(2)}) async-start(bf16[3,1,256,1024]{3,0,1,2:T(4,128)(2,1)} %maximum_bitcast_fusion), calls=%async_computation | async-start | bytes 4194304 | tf_op jit(solution)/shard_map/all_to_all | solution.py:58
  22.7 0.1 fusion.103
  22.8 48.2 %all-to-all-done = bf16[3,1,256,1024]{3,0,1,2:T(4,128)(2,1)S(1)} async-done(((bf16[3,1,256,1024]{3,0,1,2:T(4,128)(2,1)}), bf16[3,1,256,1024]{3,0,1,2:T(4,128)(2,1)S(1)}, u32[]{:S(2)}, u32[]{:S(2)}) %all-to-all-start) | async-done | bytes 1572896 | tf_op jit(solution)/shard_map/all_to_all | solution.py:58
  71.0 0.6 copy.87
  71.6 1.4 fusion.32
  73.1 1.4 fusion.29
  74.5 1.8 add_bitcast_fusion.1
  76.3 1.8 add_bitcast_fusion
  78.1 4.1 slice_bitcast_fusion.10
  82.2 4.3 multiply_subtract_fusion
  86.5 1.7 pad_maximum_fusion
  88.1 8.1 %copy.50 = f32[2,2,64,8,1024]{4,3,1,0,2:T(8,128)} copy(f32[2,2,64,8,1024]{4,2,3,1,0:T(8,128)S(1)} %pad_maximum_fusion) | data formatting | bytes 16777216 | tf_op jit(solution)/shard_map/stack | solution.py:71
  96.2 6.3 all-to-all-start.1
  102.6 0.1 cosine_multiply_fusion
  102.7 183.2 %all-to-all-done.1 = f32[2,2,64,8,1024]{4,3,1,0,2:T(8,128)} async-done(((f32[2,2,64,8,1024]{4,3,1,0,2:T(8,128)}), f32[2,2,64,8,1024]{4,3,1,0,2:T(8,128)}, u32[]{:S(2)}, u32[]{:S(2)}) %all-to-all-start.1) | async-done | bytes 8388640 | tf_op jit(solution)/shard_map/all_to_all | solution.py:70
  285.9 4.2 copy.85
  290.2 4.4 fusion.3
  294.5 4.4 fusion.2
  298.9 15.3 %subtract_bitcast_fusion = f32[2,2,256,1024]{2,3,1,0:T(8,128)S(1)} fusion(f32[2,2,1024,256]{3,2,1,0:T(8,128)S(1)} %fusion.3, f32[2,2,2,256,1024]{4,3,2,1,0:T(8,128)S(1)} %bitcast.177), kind=kOutput, calls=%fused_computation.13 | convolution fusion | flops 1612644352 | bytes 12582912 | tf_op jit(solution)/shard_map/mb,sjbc->sjmc/dot_general | solution.py:23
  314.3 4.5 add_bitcast_fusion.2
  318.8 0.5 multiply_subtract_fusion.1
  319.3 2.0 fusion.12
  321.3 2.0 fusion.10
  323.3 2.0 fusion.18
  325.3 2.2 subtract_bitcast_fusion.1
  327.5 2.2 pad_maximum_fusion.3
  329.7 7.4 %copy.55 = f32[2,2,256,1024]{3,1,0,2:T(2,128)} copy(f32[2,2,256,1024]{2,3,1,0:T(8,128)} %pad_maximum_fusion.3) | data formatting | bytes 8388608 | tf_op jit(solution)/shard_map/stack | solution.py:87
  337.2 99.8 %all_to_all.54 = f32[2,2,256,1024]{3,1,0,2:T(2,128)S(1)} all-to-all(f32[2,2,256,1024]{3,1,0,2:T(2,128)} %copy.55), channel_id=1, replica_groups=mesh['pos'=32,'chan'=8] {'pos'}, dimensions={2} | all-to-all | bytes 8388608 | tf_op jit(solution)/shard_map/all_to_all | solution.py:86
  437.0 2.4 copy.86
  439.4 1.8 fusion.169
  441.2 1.6 copy.57
  442.9 2.5 squeeze.14
  445.3 0.0 copy-start
  445.3 2.5 fusion.72
  447.8 0.0 copy-done
  447.8 3.0 copy.58
  450.8 2.7 squeeze.15
  453.5 0.7 fusion.27
  454.2 0.0 copy-start.1
  454.2 1.1 copy.59
  455.3 0.0 copy-start.3
  455.3 6.1 all-to-all-start.3
  461.4 0.0 reduce-scatter.2.cloned.1.call-start
  461.4 0.0 copy-done.1
  461.4 0.7 copy.60
  462.1 0.7 slice_bitcast_fusion.13
  462.9 0.0 copy-done.3
  462.9 0.6 fusion.24
  463.5 0.1 fusion.34
  463.6 12.6 %all-to-all-done.3 = bf16[32,8,1024]{2,1,0:T(8,128)(2,1)} async-done(((bf16[32,8,1024]{2,1,0:T(8,128)(2,1)}), bf16[32,8,1024]{2,1,0:T(8,128)(2,1)}, u32[]{:S(2)}, u32[]{:S(2)}) %all-to-all-start.3) | async-done | bytes 524320 | tf_op jit(solution)/shard_map/all_to_all | solution.py:93
  476.1 0.7 slice.189
  476.9 120.4 %psum.7 = bf16[8,1024]{1,0:T(8,128)(2,1)S(1)} all-reduce(bf16[8,1024]{1,0:T(8,128)(2,1)S(1)} %maximum_select_fusion), channel_id=1, replica_groups=mesh['pos'=32,'chan'=8] {'pos'}, use_global_device_ids=true, to_apply=%region_0.1 | all-reduce | flops 8192 | bytes 32768 | tf_op jit(solution)/shard_map/psum | solution.py:13
  597.3 0.1 multiply_add_fusion.2
  597.4 6.0 fusion
  603.4 0.0 reduce-scatter.2.cloned.1.call-update
  603.4 111.8 %reduce-scatter.2.cloned.1.call-done = f32[32,4,512]{2,0,1:T(8,128)} async-done(((f32[32,4,4096]{2,0,1:T(8,128)}), f32[32,4,512]{2,0,1:T(8,128)}) %reduce-scatter.2.cloned.1.call-update) | async-done | bytes 262160 | tf_op jit(solution)/shard_map/reduce_scatter | solution.py:122
  715.3 1.0 convert_element_type.125
  716.3 0.8 copy.62
  717.0 1.9 copy.89
  (8 shorter events, 0.1 us)
Async XLA Ops:
  7.2 2.0 copy-start.2
  13.4 57.6 %all-to-all-start = ((bf16[3,1,256,1024]{3,0,1,2:T(4,128)(2,1)}), bf16[3,1,256,1024]{3,0,1,2:T(4,128)(2,1)S(1)}, u32[]{:S(2)}, u32[]{:S(2)}) async-start(bf16[3,1,256,1024]{3,0,1,2:T(4,128)(2,1)} %maximum_bitcast_fusion), calls=%async_computation | async-start | bytes 4194304 | tf_op jit(solution)/shard_map/all_to_all | solution.py:58
  96.2 189.7 %all-to-all-start.1 = ((f32[2,2,64,8,1024]{4,3,1,0,2:T(8,128)}), f32[2,2,64,8,1024]{4,3,1,0,2:T(8,128)}, u32[]{:S(2)}, u32[]{:S(2)}) async-start(f32[2,2,64,8,1024]{4,3,1,0,2:T(8,128)} %copy.50), calls=%async_computation.1 | async-start | bytes 16777216 | tf_op jit(solution)/shard_map/all_to_all | solution.py:70
  445.3 2.5 copy-start
  454.2 7.2 copy-start.1
  455.3 7.6 %copy-start.3 = (s32[32,4]{0,1:T(4,128)S(1)}, s32[32,4]{0,1:T(4,128)}, u32[]{:S(2)}) copy-start(s32[32,4]{0,1:T(4,128)} %param.7) | copy-start | bytes 1540
  455.3 20.8 %all-to-all-start.3 = ((bf16[32,8,1024]{2,1,0:T(8,128)(2,1)}), bf16[32,8,1024]{2,1,0:T(8,128)(2,1)}, u32[]{:S(2)}, u32[]{:S(2)}) async-start(bf16[32,8,1024]{2,1,0:T(8,128)(2,1)} %copy.59), calls=%async_computation.3 | async-start | bytes 1048576 | tf_op jit(solution)/shard_map/all_to_all | solution.py:93
  461.4 253.9 %reduce-scatter.2.cloned.1.call-start = ((), (), s32[]{:S(2)}) async-start(), calls=%async_computation.5 | async-start | bytes 2359296 | tf_op jit(solution)/shard_map/reduce_scatter | solution.py:122
Sparse Core Ops, SparseCore 0:
  603.6 111.6 reduce-scatter.1
where the time goes:
time: 730 us; the launch traced here: 726 us
  waiting for transfers between devices  356 us (49%)
  blocking collectives  220 us (30%)
  matrix products  53 us (7%)
  local copies, waits for them, and re-layouts  43.2 us (6%)
  starting transfers between devices  21.7 us (3%)
  other arithmetic  17.4 us (2%)
  between operations  14.6 us (2%)
    all_to_all x1, waiting for transfers between devices, per_device(): lax.all_to_all(jnp.stack([turned_re, turned_im], 1), 'pos', split_axis=2,...  183 us
    psum x1, blocking collectives, spread(): return lax.psum(jnp.where(mine, x, jnp.zeros_like(x)), axis)  120 us
    reduce_scatter x1, waiting for transfers between devices, per_device(): lax.psum_scatter(terms, 'chan', scatter_dimension=2, tiled=True)  112 us
    all_to_all x1, blocking collectives, per_device(): lax.all_to_all(jnp.stack([final_re, final_im]), 'pos', split_axis=2, conc...  99.8 us
    all_to_all x1, waiting for transfers between devices, per_device(): lax.all_to_all(stacked[:, None], 'pos', split_axis=2, concat_axis=1, tile...  48.2 us
    dot_general x10, matrix products, contract(): jnp.einsum(subscripts, matrix, operand, precision=precise, preferred_elem...  39.9 us
  transfers between devices with their start and end apart: 4, of which 4 were waited for; matrix products, arithmetic and copies ran while one was open for 0% of the time, Pallas kernels for 0%

commit v1 on v0

v1 whole, which is shorter than its diff:
```python
import functools
import math

import jax
import jax.numpy as jnp
import numpy as np
from jax import lax
from jax.experimental import pallas as pl
from jax.experimental.pallas import tpu as pltpu
from jax.sharding import PartitionSpec as P

MESH = pl.DeviceIdType.MESH
LANES = 128
GROUP = 16
F32 = jnp.float32
BF16 = jnp.bfloat16
NT = (((1,), (1,)), ((), ()))


def turn(value, cosine, sine):
    re, im = value
    near = lambda a, b: abs(a - b) < 1e-12
    if near(sine, 0.0):
        return (re, im) if cosine > 0 else (-re, -im)
    if near(cosine, 0.0):
        return (-im, re) if sine > 0 else (im, -re)
    if near(abs(cosine), abs(sine)):
        scale = abs(cosine)
        a, b = math.copysign(1, cosine), math.copysign(1, sine)
        if a > 0:
            return ((re - im if b > 0 else re + im) * scale, (im + re if b > 0 else im - re) * scale)
        return ((re + im if b > 0 else re - im) * -scale, (im - re if b > 0 else im + re) * -scale)
    return (re * cosine - im * sine, re * sine + im * cosine)


def spin(value, index, period, sign):
    angle = 2.0 * math.pi * index / period
    return turn(value, math.cos(angle), sign * math.sin(angle))


def fft(values, sign):
    size = len(values)
    if size == 1:
        return values
    even, odd = fft(values[::2], sign), fft(values[1::2], sign)
    low, high = [], []
    for k in range(size // 2):
        (er, ei), (tr, ti) = even[k], spin(odd[k], k, size, sign)
        low.append((er + tr, ei + ti))
        high.append((er - tr, ei - ti))
    return low + high


def frequency_order(blocks):
    order = [4 * q + 1 for q in range(blocks // 2)]
    size, factor = blocks, 2
    while size >= 4:
        order += [factor * (4 * q + 1) for q in range(size // 4)]
        size, factor = size // 2, factor * 2
    return order + [0, blocks]


def outer_forward(blocks, same, diff, put):
    half = blocks // 2
    held = [spin((diff(n), -diff(n + half)), n, 2 * blocks, -1) for n in range(half)]
    slot = 0
    for re, im in fft(held, -1):
        put(slot, re, im)
        slot += 1
    size = blocks
    real = [(same(n), same(n + half)) for n in range(half)]
    while size >= 4:
        half, quarter = size // 2, size // 4
        lower = [a + b for a, b in real]
        away = [a - b for a, b in real]
        held = [spin((away[n], -away[n + quarter]), n, size, -1) for n in range(quarter)]
        for re, im in fft(held, -1):
            put(slot, re, im)
            slot += 1
        real = [(lower[n], lower[n + quarter]) for n in range(quarter)]
        size = half
    first, second = real[0]
    put(slot, first + second, None)
    put(slot + 1, first - second, None)


def outer_backward(blocks, take, put):
    first, last = take(blocks - 1)[0] * 0.5, take(blocks)[0] * 0.5
    real = [first + last, first - last]
    size, start = 4, blocks - 2
    while size <= blocks:
        quarter = size // 4
        back = fft([take(start + q) for q in range(quarter)], 1)
        back = [spin(value, n, size, 1) for n, value in enumerate(back)]
        wave = [re for re, _ in back] + [-im for _, im in back]
        real = [a + b for a, b in zip(real, wave)] + [a - b for a, b in zip(real, wave)]
        size, start = size * 2, start - size // 2
    half = blocks // 2
    back = fft([take(q) for q in range(half)], 1)
    for n, value in enumerate(back):
        re, im = spin(value, n, 2 * blocks, 1)
        put(n, real[n] - re)
        put(n + half, real[n + half] + im)


def tables(blocks, rows):
    order = np.array(frequency_order(blocks))
    length = 2 * blocks * rows
    inner = np.arange(rows)
    angle = 2.0 * np.pi * (order[:, None] * inner[None, :] % length) / length
    twiddle = np.stack([np.cos(angle), -np.sin(angle)], 1).astype(np.float32)
    twiddle = np.repeat(twiddle[:, :, None, :], 8, 2)
    angle = 2.0 * np.pi * (inner[:, None] * inner[None, :] % rows) / rows
    cosine, sine = np.cos(angle), np.sin(angle)
    forward = np.block([[cosine, -sine], [sine, cosine]]).astype(np.float32)
    backward = (forward.T / (blocks * rows)).astype(np.float32)

    def split(table):
        high = table.astype(jnp.bfloat16)
        return [high, (table - high.astype(np.float32)).astype(jnp.bfloat16)]

    return twiddle, np.stack(split(forward) + split(backward))


def kernel(
    blocks, chans, zs, signal, filt, tokens, features, weight, twiddle_in, dft_in,
    contrib, decoded,
    send_x, send_f, send_g, recv_x, recv_f, recv_g, send_o, recv_o,
    work, wave, spec_x, spec_h, shifted,
    corr_send, corr_recv, seed_send, seed_recv, rows_held,
    feats, weights, twiddle, dft, query, own, gated,
    part_send, part_recv, part_own, last_send, last_recv,
    local_sem, send_sem, recv_sem,
):
    me, chan = lax.axis_index("pos"), lax.axis_index("chan")
    rows, width = signal.shape
    mine = width // blocks
    slots = blocks + 1
    chunks = mine // GROUP
    per = LANES // mine
    strips = width // LANES
    ys = chans // zs
    z_here, y_here = chan // ys, lax.rem(chan, ys)
    steps = tokens.shape[0]
    samples = tokens.shape[1]
    columns = decoded.shape[2]

    loads = [
        pltpu.make_async_copy(src, dst, local_sem.at[i])
        for i, (src, dst) in enumerate(
            ((dft_in, dft), (twiddle_in, twiddle), (features, feats), (weight, weights))
        )
    ]
    for load in loads:
        load.start()

    barrier = pltpu.get_barrier_semaphore()

    def greet(i, carry):
        pl.semaphore_signal(
            barrier, inc=1, device_id={"pos": lax.rem(me + i, blocks)}, device_id_type=MESH
        )
        return carry

    lax.fori_loop(1, blocks, greet, 0)
    for i in range(1, ys):
        there = z_here * ys + lax.rem(y_here + i, ys)
        pl.semaphore_signal(barrier, inc=1, device_id={"chan": there}, device_id_type=MESH)
    for i in range(1, zs):
        there = lax.rem(z_here + i, zs) * ys + y_here
        pl.semaphore_signal(barrier, inc=1, device_id={"chan": there}, device_id_type=MESH)

    def eye(size):
        return (
            lax.broadcasted_iota(jnp.int32, (size, size), 0)
            == lax.broadcasted_iota(jnp.int32, (size, size), 1)
        ).astype(F32).astype(BF16)

    eye_lanes, eye_rows = eye(LANES), eye(rows)

    def flipped(block):
        turned = lax.dot_general(eye_lanes, block, NT, preferred_element_type=F32)
        return turned.astype(BF16)

    for s in range(strips):
        strip = pl.ds(s * LANES, LANES)
        owners = pl.ds(s * per, per)
        send_x[owners] = flipped(signal[:, strip]).reshape(per, mine, rows)
    pl.semaphore_wait(barrier, (blocks - 1) + (ys - 1) + (zs - 1))

    def spread(source, target, slot):
        def one(i, carry):
            there = lax.rem(me + i, blocks)
            pltpu.make_async_remote_copy(
                src_ref=source(there),
                dst_ref=target,
                send_sem=send_sem.at[slot],
                recv_sem=recv_sem.at[slot],
                device_id={"pos": there},
                device_id_type=MESH,
            ).start()
            return carry

        lax.fori_loop(1, blocks, one, 0)

    def all_of(source, target, slot):
        others = pl.ds(0, blocks - 1)
        return pltpu.make_async_remote_copy(
            src_ref=source.at[others],
            dst_ref=target.at[others],
            send_sem=send_sem.at[slot],
            recv_sem=recv_sem.at[slot],
            device_id={"pos": lax.rem(me + 1, blocks)},
            device_id_type=MESH,
        )

    spread(lambda there: send_x.at[there], recv_x.at[me], 0)
    recv_x[me] = send_x[me]
    for s in range(strips):
        strip = pl.ds(s * LANES, LANES)
        send_f[pl.ds(s * per, per)] = flipped(filt[0, :, strip]).reshape(per, mine, rows)
    spread(lambda there: send_f.at[there], recv_f.at[me], 1)
    recv_f[me] = send_f[me]

    lane = lax.broadcasted_iota(jnp.int32, (1, LANES), 1)

    @pl.when(me == 0)
    def _():
        x_head = signal[0:16, :].astype(F32)
        g_head = filt[1, 0:16, :].astype(F32)
        for t in range(steps):
            row = x_head[0:1] * g_head[t : t + 1]
            for r in range(1, t + 1):
                row = row + x_head[r : r + 1] * g_head[t - r : t - r + 1]
            for s in range(strips):
                part = row[:, s * LANES : (s + 1) * LANES]
                for i in range(per):
                    shift = (t * mine - i * mine) % LANES
                    moved = pltpu.roll(part, shift, 1) if shift else part
                    inside = (lane >= t * mine) & (lane < (t + 1) * mine)
                    before = corr_send[s * per + i] if t else jnp.zeros((1, LANES), F32)
                    corr_send[s * per + i] = jnp.where(inside, moved, before)
        spread(lambda there: corr_send.at[there], corr_recv, 2)
        corr_recv[...] = corr_send[0]

    for s in range(strips):
        strip = pl.ds(s * LANES, LANES)
        turned = flipped(filt[1, :, strip]).reshape(per, chunks, GROUP, rows)
        for k in range(chunks):
            send_g[k, pl.ds(s * per, per)] = turned[:, k]
    for k in range(chunks):
        recv_g[k, me] = send_g[k, me]
    spread(lambda there: send_g.at[0, there], recv_g.at[0, me], 3)

    loads[0].wait()
    loads[1].wait()
    loads[2].wait()

    vocab = feats.shape[1]
    for t in range(steps):
        row = tokens[t : t + 1, :].astype(F32)
        where_ = lax.broadcasted_iota(jnp.int32, (samples, samples), 0) == lax.broadcasted_iota(
            jnp.int32, (samples, samples), 1
        )
        column = jnp.sum(jnp.where(where_, row, 0.0), axis=1, keepdims=True).astype(jnp.int32)
        hot = (column == lax.broadcasted_iota(jnp.int32, (samples, vocab), 1)).astype(F32).astype(BF16)
        part = pl.ds(t * samples, samples)
        query[part] = jnp.dot(hot, feats[0], preferred_element_type=F32).astype(BF16)
        own[part] = jnp.dot(hot, feats[1], preferred_element_type=F32) * jnp.dot(
            hot, feats[2], preferred_element_type=F32
        )

    def tiles(body):
        halves = rows // LANES

        def step(i, carry):
            top = pl.multiple_of((i // halves) * 8, 8)
            left = pl.multiple_of(lax.rem(i, halves) * LANES, LANES)
            body(pl.ds(top, 8), left)
            return carry

        lax.fori_loop(0, (GROUP // 8) * halves, step, 0)

    def forward_tile(same, diff):
        def body(top, left):
            across = pl.ds(left, LANES)
            imag = pl.ds(pl.multiple_of(left + rows, LANES), LANES)

            def put(slot, re, im):
                c, s = twiddle[slot, 0, :, across], twiddle[slot, 1, :, across]
                if im is None:
                    wave[slot, top, across] = re * c
                    wave[slot, top, imag] = re * s
                else:
                    wave[slot, top, across] = re * c - im * s
                    wave[slot, top, imag] = re * s + im * c

            outer_forward(
                blocks,
                lambda n: work[same, n, top, across],
                lambda n: work[diff, n, top, across],
                put,
            )

        return body

    def backward_tile(top, left):
        across = pl.ds(left, LANES)
        imag = pl.ds(pl.multiple_of(left + rows, LANES), LANES)

        def take(slot):
            c, s = twiddle[slot, 0, :, across], twiddle[slot, 1, :, across]
            re, im = wave[slot, top, across], wave[slot, top, imag]
            return re * c + im * s, im * c - re * s

        def put(n, value):
            work[0, n, top, across] = value

        outer_backward(blocks, take, put)

    group = max(g for g in range(1, 12) if slots % g == 0)

    def split(value):
        high = value.astype(BF16)
        return high, (value - high.astype(F32)).astype(BF16)

    def inner(value, table):
        high, low = split(value)
        dot = functools.partial(jnp.dot, preferred_element_type=F32)
        return dot(high, dft[table]) + dot(low, dft[table]) + dot(high, dft[table + 1])

    def by_slots(body):
        def step(i, carry):
            body(pl.ds(i * group, group))
            return carry

        lax.fori_loop(0, slots // group, step, 0)

    flat = (group * GROUP, 2 * rows)
    deep = (group, GROUP, 2 * rows)

    all_of(send_x, recv_x, 0).wait_recv()
    for k in range(chunks):
        part = pl.ds(k * GROUP, GROUP)

        def widen(n, carry):
            work[0, n] = recv_x[n, part, :].astype(F32)
            return carry

        lax.fori_loop(0, blocks, widen, 0)
        tiles(forward_tile(0, 0))

        def to_spectrum(which, k=k):
            spec_x[k, which] = inner(wave[which].reshape(flat), 0).reshape(deep)

        by_slots(to_spectrum)

    row_id = lax.broadcasted_iota(jnp.int32, (rows, rows), 0)
    col_id = lax.broadcasted_iota(jnp.int32, (rows, rows), 1)
    bundle = 8 if blocks % 8 == 0 else blocks
    for t in range(steps):
        back = ((row_id + col_id == t) | (row_id + col_id == t + rows)).astype(F32).astype(BF16)

        def reverse(i, carry, t=t, back=back):
            which = pl.ds(i * bundle, bundle)
            taken = recv_x[which].reshape(bundle * mine, rows)
            turned = jnp.dot(taken, back, preferred_element_type=F32).astype(BF16)
            shifted[t, which] = turned.reshape(bundle, mine, rows)
            return carry

        lax.fori_loop(0, blocks // bundle, reverse, 0)

    all_of(send_f, recv_f, 1).wait_recv()
    lanes_here = lax.broadcasted_iota(jnp.int32, (mine, LANES), 1)

    def add_block(n, sums, first):
        near = recv_f[blocks - 1 - n].astype(F32)
        if not first:
            far = recv_f[blocks - n, :, 0:LANES].astype(F32)
        result = []
        for t in range(steps):
            x = shifted[t, n].astype(F32)
            other = jnp.zeros((mine, LANES), F32) if first else far
            total = x[:, 0:LANES] * jnp.where(lanes_here > t, near[:, 0:LANES], other)
            for h in range(1, rows // LANES):
                total = total + x[:, h * LANES : (h + 1) * LANES] * near[:, h * LANES : (h + 1) * LANES]
            result.append(sums[t] + total)
        return tuple(result)

    sums = add_block(0, tuple(jnp.zeros((mine, LANES), F32) for _ in range(steps)), True)
    sums = lax.fori_loop(1, blocks, lambda n, c: add_block(n, c, False), sums)
    channel = lax.broadcasted_iota(jnp.int32, (mine, LANES), 0)
    head = recv_f[0, :, 0:LANES].astype(F32)
    seed_rows = jnp.zeros((mine, LANES), F32)
    head_rows = jnp.zeros((mine, LANES), F32)
    for t in range(steps):
        place = lanes_here == t * mine + channel
        seed_rows += jnp.where(place, jnp.sum(sums[t], axis=1, keepdims=True), 0.0)
        value = jnp.sum(jnp.where(lanes_here == t, head, 0.0), axis=1, keepdims=True)
        head_rows += jnp.where(place, value, 0.0)

    @pl.when(me != 0)
    def _():
        pltpu.make_async_remote_copy(
            src_ref=corr_send.at[0], dst_ref=corr_recv, send_sem=send_sem.at[2],
            recv_sem=recv_sem.at[2], device_id={"pos": 0}, device_id_type=MESH,
        ).wait_recv()

    seed_row = jnp.sum(seed_rows, axis=0, keepdims=True) + corr_recv[...]
    seed_send[:, 0:LANES] = seed_row.astype(BF16).astype(F32)
    seed_send[:, LANES : 2 * LANES] = jnp.sum(head_rows, axis=0, keepdims=True)
    spread(lambda there: seed_send, seed_recv.at[me], 4)
    seed_recv[me] = seed_send[...]
    for k in range(1, chunks):
        spread(lambda there, k=k: send_g.at[k, there], recv_g.at[k, me], 3 + 2 * k)

    def convolve(k):
        slot = 3 + 2 * k
        all_of(send_g.at[k], recv_g.at[k], slot).wait_recv()
        part = pl.ds(k * GROUP, GROUP)

        def widen(n, carry):
            early, late = recv_f[n, part, :].astype(F32), recv_g[k, n].astype(F32)
            work[0, n] = early + late
            work[1, n] = early - late
            return carry

        lax.fori_loop(0, blocks, widen, 0)
        tiles(forward_tile(0, 1))

        def through(which):
            h = inner(wave[which].reshape(flat), 0)
            x = spec_x[k, which].reshape(flat)
            hr, hi, xr, xi = h[:, :rows], h[:, rows:], x[:, :rows], x[:, rows:]
            spec_h[:, 0:rows] = hr * xr - hi * xi
            spec_h[:, rows : 2 * rows] = hr * xi + hi * xr
            wave[which] = inner(spec_h[...], 2).reshape(deep)

        by_slots(through)
        tiles(backward_tile)

        def narrow(n, carry):
            send_o[n, k] = work[0, n].astype(BF16)
            return carry

        lax.fori_loop(0, blocks, narrow, 0)
        spread(lambda there: send_o.at[there, k], recv_o.at[me, k], 6 + 2 * k)
        recv_o[me, k] = send_o[me, k]

    def decode():
        all_of(seed_recv, seed_recv, 4).wait_recv()
        which = lax.broadcasted_iota(jnp.int32, (blocks, LANES), 1) // mine
        mod = lax.rem(lax.broadcasted_iota(jnp.int32, (blocks, LANES), 0), per)
        pick = (
            lax.broadcasted_iota(jnp.int32, (strips, blocks), 1) // per
            == lax.broadcasted_iota(jnp.int32, (strips, blocks), 0)
        ).astype(F32).astype(BF16)
        for part in range(2):
            taken = seed_recv[:, 0, part * LANES : (part + 1) * LANES]
            for t in range(steps):
                lined = jnp.zeros((blocks, LANES), F32)
                for i in range(per):
                    shift = ((i - t) * mine) % LANES
                    moved = pltpu.roll(taken, shift, 1) if shift else taken
                    lined = jnp.where((which == i) & (mod == i), moved, lined)
                rows_held[part * steps + t] = jnp.dot(
                    pick, lined.astype(BF16), preferred_element_type=F32
                )
        loads[3].wait()

        for s in range(strips):
            strip = pl.ds(s * LANES, LANES)
            for t in range(steps):
                total = jnp.broadcast_to(rows_held[t, s : s + 1, :], (samples, LANES))
                for r in range(t + 1):
                    lag = rows_held[steps + t - r, s : s + 1, :]
                    total = total + lag * own[pl.ds(r * samples, samples), strip]
                part = pl.ds(t * samples, samples)
                gated[part, strip] = (query[part, strip].astype(F32) * total).astype(BF16)

        def product(z, y):
            start = pl.multiple_of((z * ys + y) * columns, LANES)
            return jnp.dot(
                gated[...], weights[:, pl.ds(start, columns)], preferred_element_type=F32
            )

        def to_y(i, carry):
            there = lax.rem(y_here + i, ys)
            for z in range(zs):
                part_send[there, z] = product(z, there).astype(BF16)
            pltpu.make_async_remote_copy(
                src_ref=part_send.at[there], dst_ref=part_recv.at[y_here], send_sem=send_sem.at[7],
                recv_sem=recv_sem.at[7], device_id={"chan": z_here * ys + there}, device_id_type=MESH,
            ).start()
            return carry

        if ys > 1:
            lax.fori_loop(1, ys, to_y, 0)
        for z in range(zs):
            part_own[z] = product(z, y_here)

    y_all = None
    if ys > 1:
        others = pl.ds(0, ys - 1)
        y_all = pltpu.make_async_remote_copy(
            src_ref=part_send.at[others], dst_ref=part_recv.at[others], send_sem=send_sem.at[7],
            recv_sem=recv_sem.at[7], device_id={"chan": z_here * ys + lax.rem(y_here + 1, ys)},
            device_id_type=MESH,
        )
    z_copy = pltpu.make_async_remote_copy(
        src_ref=last_send, dst_ref=last_recv, send_sem=send_sem.at[9], recv_sem=recv_sem.at[9],
        device_id={"chan": lax.rem(z_here + 1, zs) * ys + y_here}, device_id_type=MESH,
    )

    def add_y():
        def one(i, carry):
            there = lax.rem(y_here + i, ys)
            for z in range(zs):
                part_own[z] += part_recv[there, z].astype(F32)
            return carry

        if ys > 1:
            y_all.wait_recv()
            lax.fori_loop(1, ys, one, 0)
        last_send[...] = part_own[1 - z_here].astype(BF16)
        z_copy.start()

    decode()
    for k in range(chunks):
        convolve(k)
        if k == 0:
            add_y()

    z_copy.wait_recv()
    result = (part_own[z_here] + last_recv[...].astype(F32)).astype(BF16)
    decoded[...] = result.reshape(steps, samples, columns)

    for k in range(chunks):
        all_of(send_o.at[:, k], recv_o.at[:, k], 6 + 2 * k).wait_recv()
    for s in range(strips):
        taken = recv_o[pl.ds(s * per, per)].reshape(LANES, rows)
        turned = lax.dot_general(eye_rows, taken, NT, preferred_element_type=F32)
        contrib[:, pl.ds(s * LANES, LANES)] = turned.astype(BF16)

    all_of(send_x, recv_x, 0).wait_send()
    all_of(send_f, recv_f, 1).wait_send()

    @pl.when(me == 0)
    def _():
        all_of(corr_send, corr_send, 2).wait_send()

    for k in range(chunks):
        all_of(send_g.at[k], recv_g.at[k], 3 + 2 * k).wait_send()
        all_of(send_o.at[:, k], recv_o.at[:, k], 6 + 2 * k).wait_send()
    all_of(seed_recv, seed_recv, 4).wait_send()
    if ys > 1:
        y_all.wait_send()
    z_copy.wait_send()


def per_device(chans, prompt_signal, long_filter, sample_tokens, token_features, out_weight):
    blocks = lax.axis_size("pos")
    rows, width = prompt_signal.shape
    samples, steps = sample_tokens.shape
    mine = width // blocks
    slots = blocks + 1
    chunks = mine // GROUP
    zs = 2
    ys = chans // zs
    columns = out_weight.shape[1] // chans
    twiddle, dft = tables(blocks, rows)
    group = max(g for g in range(1, 12) if slots % g == 0)
    vmem, dma = pltpu.VMEM, pltpu.SemaphoreType.DMA
    by_vmem = pl.BlockSpec(memory_space=pltpu.VMEM)
    by_hbm = pl.BlockSpec(memory_space=pl.ANY)
    count = steps * samples
    contributions, decoded = pl.pallas_call(
        functools.partial(kernel, blocks, chans, zs),
        out_shape=(
            jax.ShapeDtypeStruct((rows, width), BF16),
            jax.ShapeDtypeStruct((steps, samples, columns), BF16),
        ),
        in_specs=[by_vmem, by_vmem, by_vmem, by_hbm, by_hbm, by_hbm, by_hbm],
        out_specs=(by_vmem, by_vmem),
        scratch_shapes=[
            vmem((blocks, mine, rows), BF16),
            vmem((blocks, mine, rows), BF16),
            vmem((chunks, blocks, GROUP, rows), BF16),
            vmem((blocks, mine, rows), BF16),
            vmem((blocks, mine, rows), BF16),
            vmem((chunks, blocks, GROUP, rows), BF16),
            vmem((blocks, chunks, GROUP, rows), BF16),
            vmem((blocks, chunks, GROUP, rows), BF16),
            vmem((2, blocks, GROUP, rows), F32),
            vmem((slots, GROUP, 2 * rows), F32),
            vmem((chunks, slots, GROUP, 2 * rows), F32),
            vmem((group * GROUP, 2 * rows), F32),
            vmem((steps, blocks, mine, rows), BF16),
            vmem((blocks, 1, LANES), F32),
            vmem((1, LANES), F32),
            vmem((1, 2 * LANES), F32),
            vmem((blocks, 1, 2 * LANES), F32),
            vmem((2 * steps, width // LANES, LANES), F32),
            vmem((3, token_features.shape[0], width), BF16),
            vmem(out_weight.shape, BF16),
            vmem(twiddle.shape, F32),
            vmem(dft.shape, BF16),
            vmem((count, width), BF16),
            vmem((count, width), F32),
            vmem((count, width), BF16),
            vmem((ys, zs, count, columns), BF16),
            vmem((ys, zs, count, columns), BF16),
            vmem((zs, count, columns), F32),
            vmem((count, columns), BF16),
            vmem((count, columns), BF16),
            dma((4,)),
            dma((10,)),
            dma((10,)),
        ],
        compiler_params=pltpu.CompilerParams(
            collective_id=0, has_side_effects=True, vmem_limit_bytes=50 * 2**20
        ),
        name="conv_decode",
    )(
        prompt_signal,
        long_filter,
        sample_tokens.T,
        jnp.transpose(token_features, (1, 0, 2)),
        out_weight,
        jnp.asarray(twiddle),
        jnp.asarray(dft),
    )
    return contributions, jnp.transpose(decoded, (1, 0, 2))


def solution(mesh):
    placed = (
        P("pos", "chan"),
        P(None, "pos", "chan"),
        P("pos", None),
        P(None, None, "chan"),
        P("chan", None),
    )
    return jax.shard_map(
        functools.partial(per_device, mesh.shape["chan"]),
        mesh=mesh,
        in_specs=placed,
        out_specs=(P("pos", "chan"), P("pos", None, "chan")),
        check_vma=False,
    )
```

time: 730 us -> 80.5 us (0.11)
  waiting for transfers between devices: 356 us -> 0 us
  blocking collectives: 220 us -> 0 us
  Pallas kernels: 0 us -> 73.2 us
  matrix products: 53 us -> 0 us
  local copies, waits for them, and re-layouts: 43.2 us -> 5.54 us
  starting transfers between devices: 21.7 us -> 0 us
  other arithmetic: 17.4 us -> 0 us
  between operations: 14.6 us -> 0.65 us
    all_to_all x3 -> x0, waiting for transfers between devices: 244 us -> none  [the longest x1 183 us: per_device(): lax.all_to_all(jnp.stack([turned_re, turned_im], 1), 'pos', split_axis=2,...]
    psum x1 -> x0, blocking collectives: 120 us -> none  [spread(): return lax.psum(jnp.where(mine, x, jnp.zeros_like(x)), axis)]
    reduce_scatter x1 -> x0, waiting for transfers between devices: 112 us -> none  [per_device(): lax.psum_scatter(terms, 'chan', scatter_dimension=2, tiled=True)]
    all_to_all x1 -> x0, blocking collectives: 99.8 us -> none  [per_device(): lax.all_to_all(jnp.stack([final_re, final_im]), 'pos', split_axis=2, conc...]
    pallas_call x0 -> x1, Pallas kernels: none -> 73.2 us  [per_device(): pl.pallas_call(functools.partial(kernel, blocks, chans, zs), out_shape=(j...]
    dot_general x16 -> x0, matrix products: 53 us -> none  [the longest x10 39.9 us: contract(): jnp.einsum(subscripts, matrix, operand, precision=precise, preferred_elem...]
    all_to_all x3 -> x0, starting transfers between devices: 21.6 us -> none  [the longest x1 9.28 us: per_device(): lax.all_to_all(stacked[:, None], 'pos', split_axis=2, concat_axis=1, tile...]
    another operation x2 -> x0, local copies, waits for them, and re-layouts: 15.5 us -> none  [the longest x1 8.1 us: per_device(): jnp.stack([turned_re, turned_im], 1)]
  transfers between devices with their start and end apart: 4 -> 0, of which waited for: 4 -> 0; matrix products, arithmetic and copies ran while one was open for 0% -> 0% of each run, Pallas kernels for 0% -> 0%
where the time goes in v1:
time: 80.5 us; the launch traced here: 79.4 us
  Pallas kernels  73.2 us (91%)
  local copies, waits for them, and re-layouts  5.54 us (7%)
    pallas_call x1, Pallas kernels, per_device(): pl.pallas_call(functools.partial(kernel, blocks, chans, zs), out_shape=(j...  73.2 us
    unnamed x10, local copies, waits for them, and re-layouts  5.54 us

profile of v1, /device:TPU:6, one launch (start us, length us, event | category | flops | bytes accessed | tf_op | source)
XLA Modules:
  0.0 79.4 jit_solution(4916013325355216425)
XLA Ops:
  0.6 0.0 copy-start
  0.6 1.2 %copy-done = bf16[2,256,1024]{2,1,0:T(8,128)(2,1)S(1)} copy-done((bf16[2,256,1024]{2,1,0:T(8,128)(2,1)S(1)}, bf16[2,256,1024]{2,1,0:T(8,128)(2,1)}, u32[]{:S(2)}) %copy-start) | copy-done | bytes 1048600
  1.9 0.0 copy-start.1
  1.9 1.0 %copy-done.1 = f32[33,2,8,256]{3,2,1,0:T(8,128)S(1)} copy-done((f32[33,2,8,256]{3,2,1,0:T(8,128)S(1)}, f32[33,2,8,256]{3,2,1,0:T(8,128)}, u32[]{:S(2)}) %copy-start.1) | copy-done | bytes 540696
  2.9 0.0 copy-start.2
  2.9 1.0 %copy-done.2 = bf16[256,1024]{1,0:T(8,128)(2,1)S(1)} copy-done((bf16[256,1024]{1,0:T(8,128)(2,1)S(1)}, bf16[256,1024]{1,0:T(8,128)(2,1)}, u32[]{:S(2)}) %copy-start.2) | copy-done | bytes 524312
  3.9 0.0 copy-start.3
  3.9 0.7 copy-done.3
  4.6 73.2 %conv_decode.1 = (bf16[256,1024]{1,0:T(8,128)(2,1)S(1)}, bf16[4,32,512]{2,1,0:T(8,128)(2,1)S(1)}) custom-call(bf16[256,1024]{1,0:T(8,128)(2,1)S(1)} %copy-done.2, bf16[2,256,1024]{2,1,0:T(8,128)(2,1)S(1)} %copy-done, s32[4,32]{1,0:T(4,128)S(1)} %bitcast.4, bf16[3,256,1024]{2,1,0:T(8,128)(2,1)} %bitcast.5, bf16[1024,4096]{1,0:T(8,128)(2,1)} %weight.1, ...), custom_call_target="tpu_custom_call" | custom-call | tf_op jit(solution)/shard_map/conv_decode/pallas_call | solution.py:577
  77.8 0.8 copy.9
  78.6 0.8 copy.11
Async XLA Ops:
  0.6 1.2 %copy-start = (bf16[2,256,1024]{2,1,0:T(8,128)(2,1)S(1)}, bf16[2,256,1024]{2,1,0:T(8,128)(2,1)}, u32[]{:S(2)}) copy-start(bf16[2,256,1024]{2,1,0:T(8,128)(2,1)} %filt.1) | copy-start | bytes 3145732
  1.9 1.0 %copy-start.1 = (f32[33,2,8,256]{3,2,1,0:T(8,128)S(1)}, f32[33,2,8,256]{3,2,1,0:T(8,128)}, u32[]{:S(2)}) copy-start(f32[33,2,8,256]{3,2,1,0:T(8,128)} %constant.4.clone.twiddle_in) | copy-start | bytes 1622020
  2.9 1.0 %copy-start.2 = (bf16[256,1024]{1,0:T(8,128)(2,1)S(1)}, bf16[256,1024]{1,0:T(8,128)(2,1)}, u32[]{:S(2)}) copy-start(bf16[256,1024]{1,0:T(8,128)(2,1)} %signal.1) | copy-start | bytes 1572868
  3.9 0.7 copy-start.3

commit v2 on v1

--- a/solution.py
+++ b/solution.py
@@ -105,12 +105,13 @@
 
 def tables(blocks, rows):
     order = np.array(frequency_order(blocks))
-    length = 2 * blocks * rows
-    inner = np.arange(rows)
+    length, half = 2 * blocks * rows, rows // 2
+    inner = np.arange(half)
     angle = 2.0 * np.pi * (order[:, None] * inner[None, :] % length) / length
-    twiddle = np.stack([np.cos(angle), -np.sin(angle)], 1).astype(np.float32)
-    twiddle = np.repeat(twiddle[:, :, None, :], 8, 2)
-    angle = 2.0 * np.pi * (inner[:, None] * inner[None, :] % rows) / rows
+    odd = angle + 2.0 * np.pi * inner[None, :] / rows
+    twiddle = np.stack([np.cos(angle), -np.sin(angle), np.cos(odd), -np.sin(odd)], 1)
+    twiddle = np.repeat(twiddle.astype(np.float32)[:, :, None, :], 8, 2)
+    angle = 2.0 * np.pi * (inner[:, None] * inner[None, :] % half) / half
     cosine, sine = np.cos(angle), np.sin(angle)
     forward = np.block([[cosine, -sine], [sine, cosine]]).astype(np.float32)
     backward = (forward.T / (blocks * rows)).astype(np.float32)
@@ -123,8 +124,9 @@
 
 
 def kernel(
-    blocks, chans, zs, signal, filt, tokens, features, weight, twiddle_in, dft_in,
+    blocks, chans, zs, signal_in, filt_in, tokens_in, features, weight, twiddle_in, dft_in,
     contrib, decoded,
+    signal, filt, tokens,
     send_x, send_f, send_g, recv_x, recv_f, recv_g, send_o, recv_o,
     work, wave, spec_x, spec_h, shifted,
     corr_send, corr_recv, seed_send, seed_recv, rows_held,
@@ -141,14 +143,24 @@
     strips = width // LANES
     ys = chans // zs
     z_here, y_here = chan // ys, lax.rem(chan, ys)
-    steps = tokens.shape[0]
-    samples = tokens.shape[1]
+    planes = blocks // 4
+    mirror = (3 - me // planes) * planes + lax.rem(me, planes)
+    steps = tokens.shape[1]
+    samples = tokens.shape[2]
     columns = decoded.shape[2]
 
     loads = [
         pltpu.make_async_copy(src, dst, local_sem.at[i])
         for i, (src, dst) in enumerate(
-            ((dft_in, dft), (twiddle_in, twiddle), (features, feats), (weight, weights))
+            (
+                (signal_in, signal),
+                (filt_in, filt),
+                (tokens_in, tokens.at[0]),
+                (dft_in, dft),
+                (twiddle_in, twiddle),
+                (features, feats),
+                (weight, weights),
+            )
         )
     ]
     for load in loads:
@@ -166,9 +178,10 @@
     for i in range(1, ys):
         there = z_here * ys + lax.rem(y_here + i, ys)
         pl.semaphore_signal(barrier, inc=1, device_id={"chan": there}, device_id_type=MESH)
-    for i in range(1, zs):
-        there = lax.rem(z_here + i, zs) * ys + y_here
-        pl.semaphore_signal(barrier, inc=1, device_id={"chan": there}, device_id_type=MESH)
+    across = (1 - z_here) * ys + y_here
+    pl.semaphore_signal(
+        barrier, inc=1, device_id={"pos": mirror, "chan": across}, device_id_type=MESH
+    )
 
     def eye(size):
         return (
@@ -182,11 +195,12 @@
         turned = lax.dot_general(eye_lanes, block, NT, preferred_element_type=F32)
         return turned.astype(BF16)
 
+    loads[0].wait()
     for s in range(strips):
         strip = pl.ds(s * LANES, LANES)
         owners = pl.ds(s * per, per)
         send_x[owners] = flipped(signal[:, strip]).reshape(per, mine, rows)
-    pl.semaphore_wait(barrier, (blocks - 1) + (ys - 1) + (zs - 1))
+    pl.semaphore_wait(barrier, (blocks - 1) + (ys - 1) + 1)
 
     def spread(source, target, slot):
         def one(i, carry):
@@ -216,6 +230,7 @@
 
     spread(lambda there: send_x.at[there], recv_x.at[me], 0)
     recv_x[me] = send_x[me]
+    loads[1].wait()
     for s in range(strips):
         strip = pl.ds(s * LANES, LANES)
         send_f[pl.ds(s * per, per)] = flipped(filt[0, :, strip]).reshape(per, mine, rows)
@@ -252,71 +267,96 @@
         recv_g[k, me] = send_g[k, me]
     spread(lambda there: send_g.at[0, there], recv_g.at[0, me], 3)
 
-    loads[0].wait()
-    loads[1].wait()
     loads[2].wait()
+    token_copy = pltpu.make_async_remote_copy(
+        src_ref=tokens.at[0], dst_ref=tokens.at[1], send_sem=send_sem.at[10], recv_sem=recv_sem.at[10],
+        device_id={"pos": mirror}, device_id_type=MESH,
+    )
+    token_copy.start()
+    for load in loads[3:6]:
+        load.wait()
 
     vocab = feats.shape[1]
-    for t in range(steps):
-        row = tokens[t : t + 1, :].astype(F32)
-        where_ = lax.broadcasted_iota(jnp.int32, (samples, samples), 0) == lax.broadcasted_iota(
-            jnp.int32, (samples, samples), 1
-        )
-        column = jnp.sum(jnp.where(where_, row, 0.0), axis=1, keepdims=True).astype(jnp.int32)
-        hot = (column == lax.broadcasted_iota(jnp.int32, (samples, vocab), 1)).astype(F32).astype(BF16)
-        part = pl.ds(t * samples, samples)
-        query[part] = jnp.dot(hot, feats[0], preferred_element_type=F32).astype(BF16)
-        own[part] = jnp.dot(hot, feats[1], preferred_element_type=F32) * jnp.dot(
-            hot, feats[2], preferred_element_type=F32
-        )
+    same_place = lax.broadcasted_iota(jnp.int32, (samples, samples), 0) == lax.broadcasted_iota(
+        jnp.int32, (samples, samples), 1
+    )
+    for group in range(2):
+        if group == 1:
+            token_copy.wait_recv()
+        for t in range(steps):
+            row = tokens[group, t : t + 1, :].astype(F32)
+            column = jnp.sum(jnp.where(same_place, row, 0.0), axis=1, keepdims=True).astype(jnp.int32)
+            hot = column == lax.broadcasted_iota(jnp.int32, (samples, vocab), 1)
+            hot = hot.astype(F32).astype(BF16)
+            part = pl.ds((group * steps + t) * samples, samples)
+            query[part] = jnp.dot(hot, feats[0], preferred_element_type=F32).astype(BF16)
+            own[part] = jnp.dot(hot, feats[1], preferred_element_type=F32) * jnp.dot(
+                hot, feats[2], preferred_element_type=F32
+            )
+
+    order = frequency_order(blocks)
+    half = rows // 2
 
     def tiles(body):
-        halves = rows // LANES
-
         def step(i, carry):
-            top = pl.multiple_of((i // halves) * 8, 8)
-            left = pl.multiple_of(lax.rem(i, halves) * LANES, LANES)
-            body(pl.ds(top, 8), left)
-            return carry
-
-        lax.fori_loop(0, (GROUP // 8) * halves, step, 0)
+            body(pl.ds(pl.multiple_of(i * 8, 8), 8))
+            return carry
+
+        lax.fori_loop(0, GROUP // 8, step, 0)
+
+    real, imag = pl.ds(0, half), pl.ds(half, half)
 
     def forward_tile(same, diff):
-        def body(top, left):
-            across = pl.ds(left, LANES)
-            imag = pl.ds(pl.multiple_of(left + rows, LANES), LANES)
-
-            def put(slot, re, im):
-                c, s = twiddle[slot, 0, :, across], twiddle[slot, 1, :, across]
+        def body(top):
+            def put_lower(slot, re, im):
+                wave[slot, 0, top, real] = re
+                if im is not None:
+                    wave[slot, 0, top, imag] = im
+
+            def put_upper(slot, re, im):
+                ar = wave[slot, 0, top, real]
                 if im is None:
-                    wave[slot, top, across] = re * c
-                    wave[slot, top, imag] = re * s
+                    ai = im = jnp.zeros_like(re)
                 else:
-                    wave[slot, top, across] = re * c - im * s
-                    wave[slot, top, imag] = re * s + im * c
-
-            outer_forward(
-                blocks,
-                lambda n: work[same, n, top, across],
-                lambda n: work[diff, n, top, across],
-                put,
-            )
+                    ai = wave[slot, 0, top, imag]
+                br, bi = spin((re, im), order[slot], 4 * blocks, -1)
+                for part, (vr, vi) in enumerate(((ar + br, ai + bi), (ar - br, ai - bi))):
+                    c, s = twiddle[slot, 2 * part], twiddle[slot, 2 * part + 1]
+                    wave[slot, part, top, real] = vr * c - vi * s
+                    wave[slot, part, top, imag] = vr * s + vi * c
+
+            for across, put in ((real, put_lower), (imag, put_upper)):
+                outer_forward(
+                    blocks,
+                    lambda n, across=across: work[same, n, top, across],
+                    lambda n, across=across: work[diff, n, top, across],
+                    put,
+                )
 
         return body
 
-    def backward_tile(top, left):
-        across = pl.ds(left, LANES)
-        imag = pl.ds(pl.multiple_of(left + rows, LANES), LANES)
-
-        def take(slot):
-            c, s = twiddle[slot, 0, :, across], twiddle[slot, 1, :, across]
-            re, im = wave[slot, top, across], wave[slot, top, imag]
-            return re * c + im * s, im * c - re * s
-
-        def put(n, value):
-            work[0, n, top, across] = value
-
-        outer_backward(blocks, take, put)
+    def backward_tile(top):
+        def take_lower(slot):
+            turned = []
+            for part in range(2):
+                c, s = twiddle[slot, 2 * part], twiddle[slot, 2 * part + 1]
+                re, im = wave[slot, part, top, real], wave[slot, part, top, imag]
+                turned.append((re * c + im * s, im * c - re * s))
+            (er, ei), (vr, vi) = turned
+            br, bi = spin((er - vr, ei - vi), order[slot], 4 * blocks, 1)
+            wave[slot, 0, top, real] = br
+            wave[slot, 0, top, imag] = bi
+            return er + vr, ei + vi
+
+        def take_upper(slot):
+            return wave[slot, 0, top, real], wave[slot, 0, top, imag]
+
+        for across, take in ((real, take_lower), (imag, take_upper)):
+
+            def put(n, value, across=across):
+                work[0, n, top, across] = value
+
+            outer_backward(blocks, take, put)
 
     group = max(g for g in range(1, 12) if slots % g == 0)
 
@@ -336,8 +376,8 @@
 
         lax.fori_loop(0, slots // group, step, 0)
 
-    flat = (group * GROUP, 2 * rows)
-    deep = (group, GROUP, 2 * rows)
+    flat = (group * 2 * GROUP, rows)
+    deep = (group, 2, GROUP, rows)
 
     all_of(send_x, recv_x, 0).wait_recv()
     for k in range(chunks):
@@ -431,9 +471,9 @@
         def through(which):
             h = inner(wave[which].reshape(flat), 0)
             x = spec_x[k, which].reshape(flat)
-            hr, hi, xr, xi = h[:, :rows], h[:, rows:], x[:, :rows], x[:, rows:]
-            spec_h[:, 0:rows] = hr * xr - hi * xi
-            spec_h[:, rows : 2 * rows] = hr * xi + hi * xr
+            hr, hi, xr, xi = h[:, :half], h[:, half:], x[:, :half], x[:, half:]
+            spec_h[:, real] = hr * xr - hi * xi
+            spec_h[:, imag] = hr * xi + hi * xr
             wave[which] = inner(spec_h[...], 2).reshape(deep)
 
         by_slots(through)
@@ -466,73 +506,75 @@
                 rows_held[part * steps + t] = jnp.dot(
                     pick, lined.astype(BF16), preferred_element_type=F32
                 )
-        loads[3].wait()
-
-        for s in range(strips):
-            strip = pl.ds(s * LANES, LANES)
-            for t in range(steps):
-                total = jnp.broadcast_to(rows_held[t, s : s + 1, :], (samples, LANES))
-                for r in range(t + 1):
-                    lag = rows_held[steps + t - r, s : s + 1, :]
-                    total = total + lag * own[pl.ds(r * samples, samples), strip]
-                part = pl.ds(t * samples, samples)
-                gated[part, strip] = (query[part, strip].astype(F32) * total).astype(BF16)
-
-        def product(z, y):
-            start = pl.multiple_of((z * ys + y) * columns, LANES)
-            return jnp.dot(
-                gated[...], weights[:, pl.ds(start, columns)], preferred_element_type=F32
-            )
-
-        def to_y(i, carry):
-            there = lax.rem(y_here + i, ys)
-            for z in range(zs):
-                part_send[there, z] = product(z, there).astype(BF16)
-            pltpu.make_async_remote_copy(
-                src_ref=part_send.at[there], dst_ref=part_recv.at[y_here], send_sem=send_sem.at[7],
-                recv_sem=recv_sem.at[7], device_id={"chan": z_here * ys + there}, device_id_type=MESH,
-            ).start()
-            return carry
-
-        if ys > 1:
+        loads[6].wait()
+
+        count = steps * samples
+        for group in (1, 0):
+            base = group * count
+            for s in range(strips):
+                strip = pl.ds(s * LANES, LANES)
+                for t in range(steps):
+                    total = jnp.broadcast_to(rows_held[t, s : s + 1, :], (samples, LANES))
+                    for r in range(t + 1):
+                        lag = rows_held[steps + t - r, s : s + 1, :]
+                        total = total + lag * own[pl.ds(base + r * samples, samples), strip]
+                    part = pl.ds(base + t * samples, samples)
+                    gated[part, strip] = (query[part, strip].astype(F32) * total).astype(BF16)
+            z = z_here if group == 0 else 1 - z_here
+
+            def product(y, z=z, base=base):
+                start = pl.multiple_of((z * ys + y) * columns, LANES)
+                return jnp.dot(
+                    gated[pl.ds(base, count)], weights[:, pl.ds(start, columns)],
+                    preferred_element_type=F32,
+                )
+
+            def to_y(i, carry, group=group):
+                there = lax.rem(y_here + i, ys)
+                part_send[group, there] = product(there).astype(BF16)
+                pltpu.make_async_remote_copy(
+                    src_ref=part_send.at[group, there], dst_ref=part_recv.at[group, y_here],
+                    send_sem=send_sem.at[7 + 4 * group], recv_sem=recv_sem.at[7 + 4 * group],
+                    device_id={"chan": z_here * ys + there}, device_id_type=MESH,
+                ).start()
+                return carry
+
             lax.fori_loop(1, ys, to_y, 0)
-        for z in range(zs):
-            part_own[z] = product(z, y_here)
-
-    y_all = None
-    if ys > 1:
-        others = pl.ds(0, ys - 1)
-        y_all = pltpu.make_async_remote_copy(
-            src_ref=part_send.at[others], dst_ref=part_recv.at[others], send_sem=send_sem.at[7],
-            recv_sem=recv_sem.at[7], device_id={"chan": z_here * ys + lax.rem(y_here + 1, ys)},
-            device_id_type=MESH,
+            part_own[group] = product(y_here)
+
+    others = pl.ds(0, ys - 1)
+    y_all = [
+        pltpu.make_async_remote_copy(
+            src_ref=part_send.at[group, others], dst_ref=part_recv.at[group, others],
+            send_sem=send_sem.at[7 + 4 * group], recv_sem=recv_sem.at[7 + 4 * group],
+            device_id={"chan": z_here * ys + lax.rem(y_here + 1, ys)}, device_id_type=MESH,
         )
+        for group in range(2)
+    ]
     z_copy = pltpu.make_async_remote_copy(
         src_ref=last_send, dst_ref=last_recv, send_sem=send_sem.at[9], recv_sem=recv_sem.at[9],
-        device_id={"chan": lax.rem(z_here + 1, zs) * ys + y_here}, device_id_type=MESH,
+        device_id={"pos": mirror, "chan": across}, device_id_type=MESH,
     )
 
-    def add_y():
+    def add_y(group):
         def one(i, carry):
-            there = lax.rem(y_here + i, ys)
-            for z in range(zs):
-                part_own[z] += part_recv[there, z].astype(F32)
-            return carry
-
-        if ys > 1:
-            y_all.wait_recv()
-            lax.fori_loop(1, ys, one, 0)
-        last_send[...] = part_own[1 - z_here].astype(BF16)
-        z_copy.start()
+            part_own[group] += part_recv[group, lax.rem(y_here + i, ys)].astype(F32)
+            return carry
+
+        y_all[group].wait_recv()
+        lax.fori_loop(1, ys, one, 0)
 
     decode()
     for k in range(chunks):
         convolve(k)
         if k == 0:
-            add_y()
-
+            add_y(1)
+            last_send[...] = part_own[1].astype(BF16)
+            z_copy.start()
+
+    add_y(0)
     z_copy.wait_recv()
-    result = (part_own[z_here] + last_recv[...].astype(F32)).astype(BF16)
+    result = (part_own[0] + last_recv[...].astype(F32)).astype(BF16)
     decoded[...] = result.reshape(steps, samples, columns)
 
     for k in range(chunks):
@@ -553,8 +595,9 @@
         all_of(send_g.at[k], recv_g.at[k], 3 + 2 * k).wait_send()
         all_of(send_o.at[:, k], recv_o.at[:, k], 6 + 2 * k).wait_send()
     all_of(seed_recv, seed_recv, 4).wait_send()
-    if ys > 1:
-        y_all.wait_send()
+    token_copy.wait_send()
+    for copy in y_all:
+        copy.wait_send()
     z_copy.wait_send()
 
 
@@ -580,9 +623,12 @@
             jax.ShapeDtypeStruct((rows, width), BF16),
             jax.ShapeDtypeStruct((steps, samples, columns), BF16),
         ),
-        in_specs=[by_vmem, by_vmem, by_vmem, by_hbm, by_hbm, by_hbm, by_hbm],
+        in_specs=[by_hbm] * 7,
         out_specs=(by_vmem, by_vmem),
         scratch_shapes=[
+            vmem(prompt_signal.shape, BF16),
+            vmem(long_filter.shape, BF16),
+            vmem((2, steps, samples), jnp.int32),
             vmem((blocks, mine, rows), BF16),
             vmem((blocks, mine, rows), BF16),
             vmem((chunks, blocks, GROUP, rows), BF16),
@@ -592,9 +638,9 @@
             vmem((blocks, chunks, GROUP, rows), BF16),
             vmem((blocks, chunks, GROUP, rows), BF16),
             vmem((2, blocks, GROUP, rows), F32),
-            vmem((slots, GROUP, 2 * rows), F32),
-            vmem((chunks, slots, GROUP, 2 * rows), F32),
-            vmem((group * GROUP, 2 * rows), F32),
+            vmem((slots, 2, GROUP, rows), F32),
+            vmem((chunks, slots, 2, GROUP, rows), F32),
+            vmem((group * 2 * GROUP, rows), F32),
             vmem((steps, blocks, mine, rows), BF16),
             vmem((blocks, 1, LANES), F32),
             vmem((1, LANES), F32),
@@ -605,17 +651,17 @@
             vmem(out_weight.shape, BF16),
             vmem(twiddle.shape, F32),
             vmem(dft.shape, BF16),
-            vmem((count, width), BF16),
-            vmem((count, width), F32),
-            vmem((count, width), BF16),
-            vmem((ys, zs, count, columns), BF16),
-            vmem((ys, zs, count, columns), BF16),
-            vmem((zs, count, columns), F32),
+            vmem((2 * count, width), BF16),
+            vmem((2 * count, width), F32),
+            vmem((2 * count, width), BF16),
+            vmem((2, ys, count, columns), BF16),
+            vmem((2, ys, count, columns), BF16),
+            vmem((2, count, columns), F32),
             vmem((count, columns), BF16),
             vmem((count, columns), BF16),
-            dma((4,)),
-            dma((10,)),
-            dma((10,)),
+            dma((7,)),
+            dma((12,)),
+            dma((12,)),
         ],
         compiler_params=pltpu.CompilerParams(
             collective_id=0, has_side_effects=True, vmem_limit_bytes=50 * 2**20

time: 80.5 us -> 80.5 us (level)
  Pallas kernels: 73.2 us -> 71.8 us
  local copies, waits for them, and re-layouts: 5.54 us -> 6.58 us
    pallas_call x1, Pallas kernels: 73.2 us -> 71.8 us  [per_device(): pl.pallas_call(functools.partial(kernel, blocks, chans, zs), out_shape=(j...]
    unnamed x10 -> x12, local copies, waits for them, and re-layouts: 5.54 us -> 6.58 us
where the time goes in v2:
time: 80.5 us; the launch traced here: 79.1 us
  Pallas kernels  71.8 us (89%)
  local copies, waits for them, and re-layouts  6.58 us (8%)
    pallas_call x1, Pallas kernels, per_device(): pl.pallas_call(functools.partial(kernel, blocks, chans, zs), out_shape=(j...  71.8 us
    unnamed x12, local copies, waits for them, and re-layouts  6.58 us

profile of v2, /device:TPU:6, one launch (start us, length us, event | category | flops | bytes accessed | tf_op | source)
XLA Modules:
  0.0 79.1 jit_solution(8520978814002107289)
XLA Ops:
  0.6 0.0 copy-start
  0.6 1.2 %copy-done = bf16[2,256,1024]{2,1,0:T(8,128)(2,1)S(1)} copy-done((bf16[2,256,1024]{2,1,0:T(8,128)(2,1)S(1)}, bf16[2,256,1024]{2,1,0:T(8,128)(2,1)}, u32[]{:S(2)}) %copy-start) | copy-done | bytes 1048600
  1.9 0.0 copy-start.1
  1.9 1.0 %copy-done.1 = f32[33,4,8,128]{3,2,1,0:T(8,128)S(1)} copy-done((f32[33,4,8,128]{3,2,1,0:T(8,128)S(1)}, f32[33,4,8,128]{3,2,1,0:T(8,128)}, u32[]{:S(2)}) %copy-start.1) | copy-done | bytes 540696
  2.9 0.0 copy-start.2
  2.9 1.0 %copy-done.2 = bf16[256,1024]{1,0:T(8,128)(2,1)S(1)} copy-done((bf16[256,1024]{1,0:T(8,128)(2,1)S(1)}, bf16[256,1024]{1,0:T(8,128)(2,1)}, u32[]{:S(2)}) %copy-start.2) | copy-done | bytes 524312
  3.9 0.0 copy-start.3
  3.9 1.0 %copy-done.3 = bf16[4,256,256]{2,1,0:T(8,128)(2,1)S(1)} copy-done((bf16[4,256,256]{2,1,0:T(8,128)(2,1)S(1)}, bf16[4,256,256]{2,1,0:T(8,128)(2,1)}, u32[]{:S(2)}) %copy-start.3) | copy-done | bytes 524312
  5.0 0.0 copy-start.4
  5.0 0.7 copy-done.4
  5.7 71.8 %conv_decode.1 = (bf16[256,1024]{1,0:T(8,128)(2,1)S(1)}, bf16[4,32,512]{2,1,0:T(8,128)(2,1)S(1)}) custom-call(bf16[256,1024]{1,0:T(8,128)(2,1)S(1)} %copy-done.2, bf16[2,256,1024]{2,1,0:T(8,128)(2,1)S(1)} %copy-done, s32[4,32]{1,0:T(4,128)S(1)} %bitcast.4, bf16[3,256,1024]{2,1,0:T(8,128)(2,1)} %bitcast.5, bf16[1024,4096]{1,0:T(8,128)(2,1)} %weight.1, ...), custom_call_target="tpu_custom_call" | custom-call | tf_op jit(solution)/shard_map/conv_decode/pallas_call | solution.py:620
  77.5 0.8 copy.9
  78.3 0.8 %copy.11 = bf16[256,1024]{1,0:T(8,128)(2,1)} copy(bf16[256,1024]{1,0:T(8,128)(2,1)S(1)} %get-tuple-element.10) | data formatting | bytes 1048576
Async XLA Ops:
  0.6 1.2 %copy-start = (bf16[2,256,1024]{2,1,0:T(8,128)(2,1)S(1)}, bf16[2,256,1024]{2,1,0:T(8,128)(2,1)}, u32[]{:S(2)}) copy-start(bf16[2,256,1024]{2,1,0:T(8,128)(2,1)} %filt_in.1) | copy-start | bytes 3145732
  1.9 1.0 %copy-start.1 = (f32[33,4,8,128]{3,2,1,0:T(8,128)S(1)}, f32[33,4,8,128]{3,2,1,0:T(8,128)}, u32[]{:S(2)}) copy-start(f32[33,4,8,128]{3,2,1,0:T(8,128)} %constant.4.clone.twiddle_in) | copy-start | bytes 1622020
  2.9 1.0 %copy-start.2 = (bf16[256,1024]{1,0:T(8,128)(2,1)S(1)}, bf16[256,1024]{1,0:T(8,128)(2,1)}, u32[]{:S(2)}) copy-start(bf16[256,1024]{1,0:T(8,128)(2,1)} %signal_in.1) | copy-start | bytes 1572868
  3.9 1.0 %copy-start.3 = (bf16[4,256,256]{2,1,0:T(8,128)(2,1)S(1)}, bf16[4,256,256]{2,1,0:T(8,128)(2,1)}, u32[]{:S(2)}) copy-start(bf16[4,256,256]{2,1,0:T(8,128)(2,1)} %constant.5.clone.dft_in) | copy-start | bytes 1572868
  5.0 0.7 copy-start.4

commit v3 on v2

--- a/solution.py
+++ b/solution.py
@@ -128,7 +128,7 @@
     contrib, decoded,
     signal, filt, tokens,
     send_x, send_f, send_g, recv_x, recv_f, recv_g, send_o, recv_o,
-    work, wave, spec_x, spec_h, shifted,
+    work, wave, spec_x, spec_h, shifted, reversal,
     corr_send, corr_recv, seed_send, seed_recv, rows_held,
     feats, weights, twiddle, dft, query, own, gated,
     part_send, part_recv, part_own, last_send, last_recv,
@@ -163,9 +163,6 @@
             )
         )
     ]
-    for load in loads:
-        load.start()
-
     barrier = pltpu.get_barrier_semaphore()
 
     def greet(i, carry):
@@ -183,6 +180,8 @@
         barrier, inc=1, device_id={"pos": mirror, "chan": across}, device_id_type=MESH
     )
 
+    loads[0].start()
+
     def eye(size):
         return (
             lax.broadcasted_iota(jnp.int32, (size, size), 0)
@@ -196,29 +195,36 @@
         return turned.astype(BF16)
 
     loads[0].wait()
+    for load in loads[1:]:
+        load.start()
+    row_id = lax.broadcasted_iota(jnp.int32, (rows, rows), 0)
+    col_id = lax.broadcasted_iota(jnp.int32, (rows, rows), 1)
+    for t in range(steps):
+        back = (row_id + col_id == t) | (row_id + col_id == t + rows)
+        reversal[:, t * rows : (t + 1) * rows] = back.astype(F32).astype(BF16)
     for s in range(strips):
         strip = pl.ds(s * LANES, LANES)
         owners = pl.ds(s * per, per)
         send_x[owners] = flipped(signal[:, strip]).reshape(per, mine, rows)
     pl.semaphore_wait(barrier, (blocks - 1) + (ys - 1) + 1)
 
-    def spread(source, target, slot):
+    def spread(source, target, slot, start=1, stop=blocks, sent=None):
         def one(i, carry):
             there = lax.rem(me + i, blocks)
             pltpu.make_async_remote_copy(
                 src_ref=source(there),
                 dst_ref=target,
-                send_sem=send_sem.at[slot],
+                send_sem=send_sem.at[slot if sent is None else sent],
                 recv_sem=recv_sem.at[slot],
                 device_id={"pos": there},
                 device_id_type=MESH,
             ).start()
             return carry
 
-        lax.fori_loop(1, blocks, one, 0)
-
-    def all_of(source, target, slot):
-        others = pl.ds(0, blocks - 1)
+        lax.fori_loop(start, stop, one, 0)
+
+    def all_of(source, target, slot, count=blocks - 1):
+        others = pl.ds(0, count)
         return pltpu.make_async_remote_copy(
             src_ref=source.at[others],
             dst_ref=target.at[others],
@@ -228,13 +234,30 @@
             device_id_type=MESH,
         )
 
+    ahead = max(blocks // 4, 1)
+    low = blocks // 2 - ahead // 2
+    high = low + ahead
+
+    def spread_ahead(source, target, slot, sent):
+        spread(source, target, slot, low, high, sent)
+
+    def spread_rest(source, target, slot):
+        spread(source, target, slot, 1, low)
+        spread(source, target, slot, high, blocks)
+
+    def rest_of(source, target, slot):
+        return all_of(source, target, slot, blocks - 1 - ahead)
+
+    def ahead_of(source, target, sent):
+        return all_of(source, target, sent, ahead)
+
     spread(lambda there: send_x.at[there], recv_x.at[me], 0)
     recv_x[me] = send_x[me]
     loads[1].wait()
     for s in range(strips):
         strip = pl.ds(s * LANES, LANES)
         send_f[pl.ds(s * per, per)] = flipped(filt[0, :, strip]).reshape(per, mine, rows)
-    spread(lambda there: send_f.at[there], recv_f.at[me], 1)
+    spread_ahead(lambda there: send_f.at[there], recv_f.at[me], 1, 12)
     recv_f[me] = send_f[me]
 
     lane = lax.broadcasted_iota(jnp.int32, (1, LANES), 1)
@@ -265,7 +288,6 @@
             send_g[k, pl.ds(s * per, per)] = turned[:, k]
     for k in range(chunks):
         recv_g[k, me] = send_g[k, me]
-    spread(lambda there: send_g.at[0, there], recv_g.at[0, me], 3)
 
     loads[2].wait()
     token_copy = pltpu.make_async_remote_copy(
@@ -379,7 +401,23 @@
     flat = (group * 2 * GROUP, rows)
     deep = (group, 2, GROUP, rows)
 
+    all_of(send_x, recv_x, 0).wait_send()
+    spread_rest(lambda there: send_f.at[there], recv_f.at[me], 1)
+    spread_ahead(lambda there: send_g.at[0, there], recv_g.at[0, me], 3, 13)
+
     all_of(send_x, recv_x, 0).wait_recv()
+    bundle = 8 if blocks % 8 == 0 else blocks
+
+    def reverse(i, carry):
+        which = pl.ds(i * bundle, bundle)
+        taken = recv_x[which].reshape(bundle * mine, rows)
+        turned = jnp.dot(taken, reversal[...], preferred_element_type=F32).astype(BF16)
+        for t in range(steps):
+            part = turned[:, t * rows : (t + 1) * rows]
+            shifted[t, which] = part.reshape(bundle, mine, rows)
+        return carry
+
+    lax.fori_loop(0, blocks // bundle, reverse, 0)
     for k in range(chunks):
         part = pl.ds(k * GROUP, GROUP)
 
@@ -395,21 +433,8 @@
 
         by_slots(to_spectrum)
 
-    row_id = lax.broadcasted_iota(jnp.int32, (rows, rows), 0)
-    col_id = lax.broadcasted_iota(jnp.int32, (rows, rows), 1)
-    bundle = 8 if blocks % 8 == 0 else blocks
-    for t in range(steps):
-        back = ((row_id + col_id == t) | (row_id + col_id == t + rows)).astype(F32).astype(BF16)
-
-        def reverse(i, carry, t=t, back=back):
-            which = pl.ds(i * bundle, bundle)
-            taken = recv_x[which].reshape(bundle * mine, rows)
-            turned = jnp.dot(taken, back, preferred_element_type=F32).astype(BF16)
-            shifted[t, which] = turned.reshape(bundle, mine, rows)
-            return carry
-
-        lax.fori_loop(0, blocks // bundle, reverse, 0)
-
+    rest_of(send_f, recv_f, 1).wait_send()
+    spread_rest(lambda there: send_g.at[0, there], recv_g.at[0, me], 3)
     all_of(send_f, recv_f, 1).wait_recv()
     lanes_here = lax.broadcasted_iota(jnp.int32, (mine, LANES), 1)
 
@@ -564,14 +589,13 @@
         y_all[group].wait_recv()
         lax.fori_loop(1, ys, one, 0)
 
+    convolve(0)
     decode()
-    for k in range(chunks):
+    for k in range(1, chunks):
         convolve(k)
-        if k == 0:
-            add_y(1)
-            last_send[...] = part_own[1].astype(BF16)
-            z_copy.start()
-
+    add_y(1)
+    last_send[...] = part_own[1].astype(BF16)
+    z_copy.start()
     add_y(0)
     z_copy.wait_recv()
     result = (part_own[0] + last_recv[...].astype(F32)).astype(BF16)
@@ -584,15 +608,17 @@
         turned = lax.dot_general(eye_rows, taken, NT, preferred_element_type=F32)
         contrib[:, pl.ds(s * LANES, LANES)] = turned.astype(BF16)
 
-    all_of(send_x, recv_x, 0).wait_send()
-    all_of(send_f, recv_f, 1).wait_send()
+    ahead_of(send_f, recv_f, 12).wait_send()
+    ahead_of(send_g.at[0], recv_g.at[0], 13).wait_send()
+    rest_of(send_g.at[0], recv_g.at[0], 3).wait_send()
 
     @pl.when(me == 0)
     def _():
         all_of(corr_send, corr_send, 2).wait_send()
 
     for k in range(chunks):
-        all_of(send_g.at[k], recv_g.at[k], 3 + 2 * k).wait_send()
+        if k > 0:
+            all_of(send_g.at[k], recv_g.at[k], 3 + 2 * k).wait_send()
         all_of(send_o.at[:, k], recv_o.at[:, k], 6 + 2 * k).wait_send()
     all_of(seed_recv, seed_recv, 4).wait_send()
     token_copy.wait_send()
@@ -642,6 +668,7 @@
             vmem((chunks, slots, 2, GROUP, rows), F32),
             vmem((group * 2 * GROUP, rows), F32),
             vmem((steps, blocks, mine, rows), BF16),
+            vmem((rows, steps * rows), BF16),
             vmem((blocks, 1, LANES), F32),
             vmem((1, LANES), F32),
             vmem((1, 2 * LANES), F32),
@@ -660,11 +687,11 @@
             vmem((count, columns), BF16),
             vmem((count, columns), BF16),
             dma((7,)),
-            dma((12,)),
-            dma((12,)),
+            dma((14,)),
+            dma((14,)),
         ],
         compiler_params=pltpu.CompilerParams(
-            collective_id=0, has_side_effects=True, vmem_limit_bytes=50 * 2**20
+            collective_id=0, has_side_effects=True, vmem_limit_bytes=60 * 2**20
         ),
         name="conv_decode",
     )(

time: 80.5 us -> 69.7 us (0.87)
  Pallas kernels: 71.8 us -> 64.6 us
  local copies, waits for them, and re-layouts: 6.58 us -> 3.53 us
    pallas_call x1, Pallas kernels: 71.8 us -> 64.6 us  [per_device(): pl.pallas_call(functools.partial(kernel, blocks, chans, zs), out_shape=(j...]
    unnamed x12 -> x2, local copies, waits for them, and re-layouts: 6.58 us -> 3.53 us
where the time goes in v3:
time: 69.7 us; the launch traced here: 68.8 us
  Pallas kernels  64.6 us (93%)
  local copies, waits for them, and re-layouts  3.53 us (5%)
    pallas_call x1, Pallas kernels, per_device(): pl.pallas_call(functools.partial(kernel, blocks, chans, zs), out_shape=(j...  64.6 us
    unnamed x2, local copies, waits for them, and re-layouts  3.53 us

profile of v3, /device:TPU:6, one launch (start us, length us, event | category | flops | bytes accessed | tf_op | source)
XLA Modules:
  0.0 68.8 jit_solution(8494262108184857516)
XLA Ops:
  0.6 64.6 %conv_decode.1 = (bf16[256,1024]{1,0:T(8,128)(2,1)}, bf16[4,32,512]{2,1,0:T(8,128)(2,1)}) custom-call(bf16[256,1024]{1,0:T(8,128)(2,1)} %signal_in.1, bf16[2,256,1024]{2,1,0:T(8,128)(2,1)} %filt_in.1, s32[4,32]{1,0:T(4,128)} %bitcast.5, bf16[3,256,1024]{2,1,0:T(8,128)(2,1)} %bitcast.3, bf16[1024,4096]{1,0:T(8,128)(2,1)} %weight.1, ...), custom_call_target="tpu_custom_call" | custom-call | tf_op jit(solution)/shard_map/conv_decode/pallas_call | solution.py:646
  65.2 1.7 %copy.9 = bf16[32,4,512]{2,1,0:T(4,128)(2,1)} copy(bf16[32,4,512]{2,0,1:T(8,128)(2,1)} %bitcast.4) | data formatting | bytes 262144
  66.9 1.9 %copy.11 = bf16[256,1024]{1,0:T(8,128)(2,1)} copy(bf16[256,1024]{1,0:T(8,128)(2,1)} %get-tuple-element.10) | data formatting | bytes 1048576

commit v4 on v3

--- a/solution.py
+++ b/solution.py
@@ -125,9 +125,9 @@
 
 def kernel(
     blocks, chans, zs, signal_in, filt_in, tokens_in, features, weight, twiddle_in, dft_in,
-    contrib, decoded,
+    recv_o, decoded,
     signal, filt, tokens,
-    send_x, send_f, send_g, recv_x, recv_f, recv_g, send_o, recv_o,
+    send_x, send_f, send_g, recv_x, recv_f, recv_g, send_o,
     work, wave, spec_x, spec_h, shifted, reversal,
     corr_send, corr_recv, seed_send, seed_recv, rows_held,
     feats, weights, twiddle, dft, query, own, gated,
@@ -144,10 +144,11 @@
     ys = chans // zs
     z_here, y_here = chan // ys, lax.rem(chan, ys)
     planes = blocks // 4
+    stride = 5
     mirror = (3 - me // planes) * planes + lax.rem(me, planes)
     steps = tokens.shape[1]
     samples = tokens.shape[2]
-    columns = decoded.shape[2]
+    columns = decoded.shape[1]
 
     loads = [
         pltpu.make_async_copy(src, dst, local_sem.at[i])
@@ -188,7 +189,7 @@
             == lax.broadcasted_iota(jnp.int32, (size, size), 1)
         ).astype(F32).astype(BF16)
 
-    eye_lanes, eye_rows = eye(LANES), eye(rows)
+    eye_lanes = eye(LANES)
 
     def flipped(block):
         turned = lax.dot_general(eye_lanes, block, NT, preferred_element_type=F32)
@@ -210,7 +211,7 @@
 
     def spread(source, target, slot, start=1, stop=blocks, sent=None):
         def one(i, carry):
-            there = lax.rem(me + i, blocks)
+            there = lax.rem(me + stride * i, blocks)
             pltpu.make_async_remote_copy(
                 src_ref=source(there),
                 dst_ref=target,
@@ -234,30 +235,29 @@
             device_id_type=MESH,
         )
 
-    ahead = max(blocks // 4, 1)
-    low = blocks // 2 - ahead // 2
-    high = low + ahead
-
-    def spread_ahead(source, target, slot, sent):
-        spread(source, target, slot, low, high, sent)
-
-    def spread_rest(source, target, slot):
-        spread(source, target, slot, 1, low)
-        spread(source, target, slot, high, blocks)
-
-    def rest_of(source, target, slot):
-        return all_of(source, target, slot, blocks - 1 - ahead)
-
-    def ahead_of(source, target, sent):
-        return all_of(source, target, sent, ahead)
-
-    spread(lambda there: send_x.at[there], recv_x.at[me], 0)
+    step_ = max(blocks // 4, 1)
+    first, second = 1 + step_, 1 + 3 * step_
+
+    def left(source, target, slot, count):
+        if count:
+            all_of(source, target, slot, count).wait_send()
+
+    def spread_x(start, stop, wave_):
+        spread(lambda there: send_x.at[there], recv_x.at[me], 0, start, stop, wave_)
+
+    def spread_f(start, stop, wave_):
+        spread(lambda there: send_f.at[there], recv_f.at[me], 1, start, stop, wave_)
+
+    def spread_g(start, stop, wave_):
+        spread(lambda there: send_g.at[0, there], recv_g.at[0, me], 3, start, stop, wave_)
+
+    spread_x(1, first, 12)
+    spread_x(first, second, 13)
     recv_x[me] = send_x[me]
     loads[1].wait()
     for s in range(strips):
         strip = pl.ds(s * LANES, LANES)
         send_f[pl.ds(s * per, per)] = flipped(filt[0, :, strip]).reshape(per, mine, rows)
-    spread_ahead(lambda there: send_f.at[there], recv_f.at[me], 1, 12)
     recv_f[me] = send_f[me]
 
     lane = lax.broadcasted_iota(jnp.int32, (1, LANES), 1)
@@ -289,6 +289,10 @@
     for k in range(chunks):
         recv_g[k, me] = send_g[k, me]
 
+    left(send_x, recv_x, 12, step_)
+    spread_x(second, blocks, 14)
+    spread_f(1, first, 14)
+
     loads[2].wait()
     token_copy = pltpu.make_async_remote_copy(
         src_ref=tokens.at[0], dst_ref=tokens.at[1], send_sem=send_sem.at[10], recv_sem=recv_sem.at[10],
@@ -401,9 +405,11 @@
     flat = (group * 2 * GROUP, rows)
     deep = (group, 2, GROUP, rows)
 
-    all_of(send_x, recv_x, 0).wait_send()
-    spread_rest(lambda there: send_f.at[there], recv_f.at[me], 1)
-    spread_ahead(lambda there: send_g.at[0, there], recv_g.at[0, me], 3, 13)
+    left(send_x, recv_x, 13, 2 * step_)
+    spread_f(first, second, 15)
+    left(send_x, recv_x, 14, blocks - second + step_)
+    spread_f(second, blocks, 16)
+    spread_g(1, first + step_, 17)
 
     all_of(send_x, recv_x, 0).wait_recv()
     bundle = 8 if blocks % 8 == 0 else blocks
@@ -433,8 +439,8 @@
 
         by_slots(to_spectrum)
 
-    rest_of(send_f, recv_f, 1).wait_send()
-    spread_rest(lambda there: send_g.at[0, there], recv_g.at[0, me], 3)
+    left(send_f, recv_f, 15, 2 * step_)
+    spread_g(first + step_, blocks, 17)
     all_of(send_f, recv_f, 1).wait_recv()
     lanes_here = lax.broadcasted_iota(jnp.int32, (mine, LANES), 1)
 
@@ -479,6 +485,9 @@
     for k in range(1, chunks):
         spread(lambda there, k=k: send_g.at[k, there], recv_g.at[k, me], 3 + 2 * k)
 
+    def kept_o(k):
+        return pltpu.make_async_copy(send_o.at[me, k], recv_o.at[me, k], local_sem.at[k])
+
     def convolve(k):
         slot = 3 + 2 * k
         all_of(send_g.at[k], recv_g.at[k], slot).wait_recv()
@@ -510,7 +519,7 @@
 
         lax.fori_loop(0, blocks, narrow, 0)
         spread(lambda there: send_o.at[there, k], recv_o.at[me, k], 6 + 2 * k)
-        recv_o[me, k] = send_o[me, k]
+        kept_o(k).start()
 
     def decode():
         all_of(seed_recv, seed_recv, 4).wait_recv()
@@ -599,18 +608,15 @@
     add_y(0)
     z_copy.wait_recv()
     result = (part_own[0] + last_recv[...].astype(F32)).astype(BF16)
-    decoded[...] = result.reshape(steps, samples, columns)
+    decoded[...] = result
 
     for k in range(chunks):
         all_of(send_o.at[:, k], recv_o.at[:, k], 6 + 2 * k).wait_recv()
-    for s in range(strips):
-        taken = recv_o[pl.ds(s * per, per)].reshape(LANES, rows)
-        turned = lax.dot_general(eye_rows, taken, NT, preferred_element_type=F32)
-        contrib[:, pl.ds(s * LANES, LANES)] = turned.astype(BF16)
-
-    ahead_of(send_f, recv_f, 12).wait_send()
-    ahead_of(send_g.at[0], recv_g.at[0], 13).wait_send()
-    rest_of(send_g.at[0], recv_g.at[0], 3).wait_send()
+    for k in range(chunks):
+        kept_o(k).wait()
+
+    left(send_f, recv_f, 16, blocks - second)
+    left(send_g.at[0], recv_g.at[0], 17, blocks - 1)
 
     @pl.when(me == 0)
     def _():
@@ -625,6 +631,28 @@
     for copy in y_all:
         copy.wait_send()
     z_copy.wait_send()
+
+
+def finish(samples, contrib_in, decoded_in, contrib, decoded):
+    rows, count = contrib_in.shape[1], decoded_in.shape[0]
+    steps = count // samples
+    here = lax.broadcasted_iota(jnp.int32, (rows, rows), 0)
+    there = lax.broadcasted_iota(jnp.int32, (rows, rows), 1)
+    same = (here == there).astype(F32).astype(BF16)
+    strip = min(rows, contrib_in.shape[0])
+    for s in range(contrib_in.shape[0] // strip):
+        part = pl.ds(s * strip, strip)
+        turned = lax.dot_general(same, contrib_in[part], NT, preferred_element_type=F32)
+        contrib[:, part] = turned.astype(BF16)
+
+    if True:
+        to = lax.broadcasted_iota(jnp.int32, (count, count), 0)
+        of = lax.broadcasted_iota(jnp.int32, (count, count), 1)
+        move = of == lax.rem(to, steps) * samples + to // steps
+        moved = jnp.dot(
+            move.astype(F32).astype(BF16), decoded_in[...], preferred_element_type=F32
+        )
+        decoded[...] = moved.reshape(decoded.shape).astype(BF16)
 
 
 def per_device(chans, prompt_signal, long_filter, sample_tokens, token_features, out_weight):
@@ -643,14 +671,14 @@
     by_vmem = pl.BlockSpec(memory_space=pltpu.VMEM)
     by_hbm = pl.BlockSpec(memory_space=pl.ANY)
     count = steps * samples
-    contributions, decoded = pl.pallas_call(
+    turned, summed = pl.pallas_call(
         functools.partial(kernel, blocks, chans, zs),
         out_shape=(
-            jax.ShapeDtypeStruct((rows, width), BF16),
-            jax.ShapeDtypeStruct((steps, samples, columns), BF16),
+            jax.ShapeDtypeStruct((blocks, chunks, GROUP, rows), BF16),
+            jax.ShapeDtypeStruct((count, columns), BF16),
         ),
         in_specs=[by_hbm] * 7,
-        out_specs=(by_vmem, by_vmem),
+        out_specs=(by_hbm, by_vmem),
         scratch_shapes=[
             vmem(prompt_signal.shape, BF16),
             vmem(long_filter.shape, BF16),
@@ -661,7 +689,6 @@
             vmem((blocks, mine, rows), BF16),
             vmem((blocks, mine, rows), BF16),
             vmem((chunks, blocks, GROUP, rows), BF16),
-            vmem((blocks, chunks, GROUP, rows), BF16),
             vmem((blocks, chunks, GROUP, rows), BF16),
             vmem((2, blocks, GROUP, rows), F32),
             vmem((slots, 2, GROUP, rows), F32),
@@ -687,8 +714,8 @@
             vmem((count, columns), BF16),
             vmem((count, columns), BF16),
             dma((7,)),
-            dma((14,)),
-            dma((14,)),
+            dma((18,)),
+            dma((18,)),
         ],
         compiler_params=pltpu.CompilerParams(
             collective_id=0, has_side_effects=True, vmem_limit_bytes=60 * 2**20
@@ -703,7 +730,16 @@
         jnp.asarray(twiddle),
         jnp.asarray(dft),
     )
-    return contributions, jnp.transpose(decoded, (1, 0, 2))
+    return pl.pallas_call(
+        functools.partial(finish, samples),
+        out_shape=(
+            jax.ShapeDtypeStruct((rows, width), BF16),
+            jax.ShapeDtypeStruct((samples, steps, columns), BF16),
+        ),
+        in_specs=[by_vmem, by_vmem],
+        out_specs=(by_vmem, by_vmem),
+        name="finish",
+    )(turned.reshape(width, rows), summed)
 
 
 def solution(mesh):

time: 69.7 us -> 67.2 us (0.964)
  local copies, waits for them, and re-layouts: 3.53 us -> 0 us
  Pallas kernels: 64.6 us -> 66 us
    unnamed x2 -> x0, local copies, waits for them, and re-layouts: 3.53 us -> none
    pallas_call x0 -> x1, Pallas kernels: none -> 2.22 us  [per_device(): pl.pallas_call(functools.partial(finish, samples), out_shape=(jax.ShapeDt...]
    pallas_call x1, Pallas kernels: 64.6 us -> 63.8 us  [per_device(): pl.pallas_call(functools.partial(kernel, blocks, chans, zs), out_shape=(j...]
where the time goes in v4:
time: 67.2 us; the launch traced here: 66.6 us
  Pallas kernels  66 us (98%)
    pallas_call x1, Pallas kernels, per_device(): pl.pallas_call(functools.partial(kernel, blocks, chans, zs), out_shape=(j...  63.8 us
    pallas_call x1, Pallas kernels, per_device(): pl.pallas_call(functools.partial(finish, samples), out_shape=(jax.ShapeDt...  2.22 us

profile of v4, /device:TPU:6, one launch (start us, length us, event | category | flops | bytes accessed | tf_op | source)
XLA Modules:
  0.0 66.6 jit_solution(121699589717948583)
XLA Ops:
  0.6 63.8 %conv_decode.1 = (bf16[32,2,16,256]{3,2,1,0:T(8,128)(2,1)}, bf16[128,512]{1,0:T(8,128)(2,1)}) custom-call(bf16[256,1024]{1,0:T(8,128)(2,1)} %signal_in.1, bf16[2,256,1024]{2,1,0:T(8,128)(2,1)} %filt_in.1, s32[4,32]{1,0:T(4,128)} %bitcast.5, bf16[3,256,1024]{2,1,0:T(8,128)(2,1)} %bitcast.3, bf16[1024,4096]{1,0:T(8,128)(2,1)} %weight.1, ...), custom_call_target="tpu_custom_call" | custom-call | tf_op jit(solution)/shard_map/conv_decode/pallas_call | solution.py:674
  64.4 2.2 %finish.1 = (bf16[256,1024]{1,0:T(8,128)(2,1)}, bf16[32,4,512]{2,1,0:T(4,128)(2,1)}) custom-call(bf16[1024,256]{1,0:T(8,128)(2,1)} %bitcast.4, bf16[128,512]{1,0:T(8,128)(2,1)} %get-tuple-element.5.decoded_in), custom_call_target="tpu_custom_call" | custom-call | tf_op jit(solution)/shard_map/finish/pallas_call | solution.py:733

commit v5 on v4

--- a/solution.py
+++ b/solution.py
@@ -384,7 +384,7 @@
 
             outer_backward(blocks, take, put)
 
-    group = max(g for g in range(1, 12) if slots % g == 0)
+    group = max(g for g in range(1, 40) if slots % g == 0)
 
     def split(value):
         high = value.astype(BF16)
@@ -393,7 +393,9 @@
     def inner(value, table):
         high, low = split(value)
         dot = functools.partial(jnp.dot, preferred_element_type=F32)
-        return dot(high, dft[table]) + dot(low, dft[table]) + dot(high, dft[table + 1])
+        both = dot(jnp.concatenate([high, low], 0), dft[table])
+        count = value.shape[0]
+        return both[:count] + both[count:] + dot(high, dft[table + 1])
 
     def by_slots(body):
         def step(i, carry):
@@ -666,7 +668,7 @@
     ys = chans // zs
     columns = out_weight.shape[1] // chans
     twiddle, dft = tables(blocks, rows)
-    group = max(g for g in range(1, 12) if slots % g == 0)
+    group = max(g for g in range(1, 40) if slots % g == 0)
     vmem, dma = pltpu.VMEM, pltpu.SemaphoreType.DMA
     by_vmem = pl.BlockSpec(memory_space=pltpu.VMEM)
     by_hbm = pl.BlockSpec(memory_space=pl.ANY)

time: 67.2 us -> 66.9 us (level)
  no operation moved by 1% of the time
where the time goes in v5:
time: 66.9 us; the launch traced here: 66.7 us
  Pallas kernels  66.1 us (99%)
    pallas_call x1, Pallas kernels, per_device(): pl.pallas_call(functools.partial(kernel, blocks, chans, zs), out_shape=(j...  63.9 us
    pallas_call x1, Pallas kernels, per_device(): pl.pallas_call(functools.partial(finish, samples), out_shape=(jax.ShapeDt...  2.23 us

profile of v5, /device:TPU:6, one launch (start us, length us, event | category | flops | bytes accessed | tf_op | source)
XLA Modules:
  0.0 66.7 jit_solution(17556701905379656457)
XLA Ops:
  0.6 63.9 %conv_decode.1 = (bf16[32,2,16,256]{3,2,1,0:T(8,128)(2,1)}, bf16[128,512]{1,0:T(8,128)(2,1)}) custom-call(bf16[256,1024]{1,0:T(8,128)(2,1)} %signal_in.1, bf16[2,256,1024]{2,1,0:T(8,128)(2,1)} %filt_in.1, s32[4,32]{1,0:T(4,128)} %bitcast.5, bf16[3,256,1024]{2,1,0:T(8,128)(2,1)} %bitcast.3, bf16[1024,4096]{1,0:T(8,128)(2,1)} %weight.1, ...), custom_call_target="tpu_custom_call" | custom-call | tf_op jit(solution)/shard_map/conv_decode/pallas_call | solution.py:676
  64.5 2.2 %finish.1 = (bf16[256,1024]{1,0:T(8,128)(2,1)}, bf16[32,4,512]{2,1,0:T(4,128)(2,1)}) custom-call(bf16[1024,256]{1,0:T(8,128)(2,1)} %bitcast.4, bf16[128,512]{1,0:T(8,128)(2,1)} %get-tuple-element.5.decoded_in), custom_call_target="tpu_custom_call" | custom-call | tf_op jit(solution)/shard_map/finish/pallas_call | solution.py:735
